TPU v7x, 32 devices: a whole 2x2x4 slice. The times are simulated.
32 devices in a mesh: lat: 2 (over x), lon: 16 (over z, y, core).
Axes of the slice: x: 2, y: 2, z: 4, core: 2. Of those that a mesh axis runs over, the one named last changes fastest.
Arguments:
- tracer: float32 [4, 512, 2048], P(None, 'lat', 'lon'), may hold values from -6 to 6
- wind_east: float32 [4, 512, 2048], P(None, 'lat', 'lon'), may hold values from -4 to 4
- wind_north: float32 [4, 512, 2048], P(None, 'lat', 'lon'), may hold values from -4 to 4
- kappa: float32 [4, 512, 2048], P(None, 'lat', 'lon'), may hold values from 0.25 to 4
- cutoff: int32 [128], replicated, may hold values from 64 to 511
- partner: int32 [2048], replicated, may hold values from 0 to 2047, as said below
Outputs:
- filtered: float32 [4, 512, 2048], P(None, 'lat', 'lon')
- balanced: float32 [4, 512, 2048], P(None, 'lat', 'lon')
Inputs may be any that keep to these rules, and one draw needn't show every extreme that they name: partner[j] = (j + 1024 + s_j) mod 2048 with each column's own shift s_j of 0 to 127; some column has s_j = 127.
All inputs are finite; a program needn't handle non-finite values.
Results may differ from a plain program's by a relative error of at most 0.00005.
Values sent between devices are 32-bit elements; how exact they have to be, the bound alone decides.
A program may use at most 64 MiB of HBM per device.

v0:
```python
import math
import jax
import jax.numpy as jnp
from jax import lax
from jax.sharding import PartitionSpec as P

KMAX = 512
SWEEPS = 4
COURANT = 0.4


def padded(cells, sides, width, closed):
    for axis, dim in sides:
        count = lax.axis_size(axis)
        ends = count if closed else count - 1
        head = lax.slice_in_dim(cells, 0, width, axis=dim)
        tail = lax.slice_in_dim(cells, cells.shape[dim] - width, cells.shape[dim], axis=dim)
        cells = jnp.concatenate(
            [
                lax.ppermute(tail, axis, [(i, (i + 1) % count) for i in range(ends)]),
                cells,
                lax.ppermute(head, axis, [((i + 1) % count, i) for i in range(ends)]),
            ],
            axis=dim,
        )
    return cells


def neighbours(field, partner):
    width = field.shape[2]
    lon_index = lax.axis_index("lon")
    lon_padded = padded(field, (("lon", 2),), 1, True)
    lat_padded = padded(field, (("lat", 1),), 1, False)
    edge_rows = jnp.stack([field[:, 0, :], field[:, -1, :]], axis=1)
    own_partner = lax.dynamic_slice_in_dim(partner, lon_index * width, width)
    whole_rows = lax.all_gather(edge_rows, "lon", axis=2, tiled=True)
    across = jnp.take(whole_rows, own_partner, axis=2)
    lat_index = lax.axis_index("lat")
    last_band = lax.axis_size("lat") - 1
    upper_row = jnp.where(lat_index == 0, across[:, 0, :], lat_padded[:, 0, :])
    lower_row = jnp.where(lat_index == last_band, across[:, 1, :], lat_padded[:, -1, :])
    upper = jnp.concatenate([upper_row[:, None, :], field[:, :-1, :]], axis=1)
    lower = jnp.concatenate([field[:, 1:, :], lower_row[:, None, :]], axis=1)
    western = lon_padded[:, :, :-2]
    eastern = lon_padded[:, :, 2:]
    return (western, eastern, upper, lower)


def tables(start, count, total, kmaximum):
    columns = start + jnp.arange(count, dtype=jnp.int32)
    waves = jnp.arange(kmaximum, dtype=jnp.int32)
    phase = columns[:, None] * waves[None, :] % total
    angle = phase.astype(jnp.float32) * (2.0 * math.pi / total)
    return (jnp.cos(angle), jnp.sin(angle))


def project(rows, start, total, kmaximum):
    cosine, sine = tables(start, rows.shape[1], total, kmaximum)
    cos_part = jnp.dot(
        rows, cosine, precision=lax.Precision.HIGHEST, preferred_element_type=jnp.float32
    )
    sin_part = jnp.dot(
        rows, sine, precision=lax.Precision.HIGHEST, preferred_element_type=jnp.float32
    )
    return (cos_part, sin_part)


def rebuild(cos_part, sin_part, limits, start, count, total):
    kmaximum = cos_part.shape[1]
    waves = jnp.arange(kmaximum, dtype=jnp.int32)
    weights = jnp.where(waves == 0, 1.0, 2.0).astype(jnp.float32) / total
    scaled = jnp.where(waves[None, :] <= limits[:, None], weights[None, :], 0.0)
    cosine, sine = tables(start, count, total, kmaximum)
    contract = (((1,), (1,)), ((), ()))
    first_term = lax.dot_general(
        cos_part * scaled,
        cosine,
        contract,
        precision=lax.Precision.HIGHEST,
        preferred_element_type=jnp.float32,
    )
    second_term = lax.dot_general(
        sin_part * scaled,
        sine,
        contract,
        precision=lax.Precision.HIGHEST,
        preferred_element_type=jnp.float32,
    )
    return first_term + second_term


def polar_filter(field, cutoff):
    levels, band_rows, width = field.shape
    pole_rows = cutoff.shape[0] // 2
    sectors = lax.axis_size("lon")
    total = width * sectors
    lon_index = lax.axis_index("lon")
    lat_index = lax.axis_index("lat")
    is_north = lat_index == 0
    is_south = lat_index == lax.axis_size("lat") - 1
    band = jnp.where(is_north, field[:, :pole_rows, :], field[:, band_rows - pole_rows :, :])
    band_limits = jnp.where(is_north, cutoff[:pole_rows], cutoff[pole_rows:])
    flat = band.reshape(levels * pole_rows, width)
    row_limits = jnp.tile(band_limits, levels)
    own_start = lon_index * width
    cos_add, sin_add = project(
        lax.all_gather(flat, "lon", axis=1, tiled=True), jnp.int32(0), total, KMAX
    )
    smooth = rebuild(cos_add, sin_add, row_limits, own_start, width, total)
    smooth = smooth.reshape(levels, pole_rows, width)
    top_rows = jnp.where(is_north, smooth, field[:, :pole_rows, :])
    bottom_rows = jnp.where(is_south, smooth, field[:, band_rows - pole_rows :, :])
    return jnp.concatenate(
        [top_rows, field[:, pole_rows : band_rows - pole_rows, :], bottom_rows], axis=1
    )


def per_device(tracer, wind_east, wind_north, kappa, cutoff, partner):
    western, eastern, upper, lower = neighbours(tracer, partner)
    advected = tracer - COURANT * 0.5 * (
        wind_east * (eastern - western) + wind_north * (lower - upper)
    )
    filtered = polar_filter(advected, cutoff)
    balanced = filtered
    for sweep_index in range(SWEEPS):
        western, eastern, upper, lower = neighbours(balanced, partner)
        balanced = (filtered + kappa * (western + eastern + upper + lower)) / (1.0 + 4.0 * kappa)
    return (filtered, balanced)


def solution(mesh):
    in_specs = (
        P(None, "lat", "lon"),
        P(None, "lat", "lon"),
        P(None, "lat", "lon"),
        P(None, "lat", "lon"),
        P(),
        P(),
    )
    out_specs = (P(None, "lat", "lon"), P(None, "lat", "lon"))
    return jax.shard_map(
        per_device, mesh=mesh, in_specs=in_specs, out_specs=out_specs, check_vma=False
    )
```

profile of v0, /device:TPU:3, one launch (start us, length us, event | category | flops | bytes accessed | tf_op | source)
XLA Modules:
  0.0 317.8 jit_solution(2903918422624642746)
XLA Ops:
  7.2 0.8 fusion.87
  8.0 1.3 collective-permute-start.2
  9.3 1.3 collective-permute-start.3
  10.6 2.3 fusion.88
  13.0 0.6 collective-permute-start
  13.6 2.3 collective-permute-start.1
  15.9 1.1 fusion.86
  16.9 0.8 compare_and_fusion
  17.7 23.6 %all_gather.18 = f32[4,2,2048]{2,0,1:T(4,128)S(1)} all-gather(f32[4,2,128]{2,0,1:T(4,128)S(1)} %pad_maximum_fusion.15), channel_id=1, replica_groups=mesh['lat'=2,'lon'=16] {'lon'}, dimensions={2}, use_global_device_ids=true | all-gather | bytes 69632 | tf_op jit(solution)/shard_map/all_gather | solution.py:36
  41.3 1.1 copy.303
  42.4 0.7 gather_fusion
  43.3 0.8 copy-done.3
  44.1 2.3 fusion.46
  46.4 0.7 slice_select_fusion.1
  47.2 0.1 le.23
  47.3 40.6 %all-gather.2.cloned.1.call-done = f32[256,2048]{1,0:T(8,128)} async-done(((f32[256,128]{1,0:T(8,128)}), f32[256,2048]{1,0:T(8,128)}) %all-gather.2.cloned.1.call-update) | async-done | bytes 2097168 | tf_op jit(solution)/shard_map/all_gather | solution.py:107
  87.8 21.2 %fusion.12 = f32[256,512]{1,0:T(8,128)S(1)} fusion(f32[256,2048]{1,0:T(8,128)} %all-gather.2.cloned.1.call-done, f32[512]{0:T(512)S(1)} %select_multiply_fusion, s32[256]{0:T(256)S(1)} %le.23), kind=kOutput, calls=%fused_computation.18 | convolution fusion | flops 3236298752 | bytes 2624512 | tf_op jit(solution)/shard_map/dot_general | solution.py:59
  109.1 1.6 fusion.52
  110.7 19.7 %fusion.15 = f32[256,512]{1,0:T(8,128)S(1)} fusion(f32[256,2048]{1,0:T(8,128)S(1)} %copy-done.5, f32[512]{0:T(512)S(1)} %select_multiply_fusion, s32[256]{0:T(256)S(1)} %le.23), kind=kOutput, calls=%fused_computation.19 | convolution fusion | flops 3236298752 | bytes 2624512 | tf_op jit(solution)/shard_map/dot_general | solution.py:62
  130.3 1.6 convolution_add_fusion
  132.0 1.1 fusion.85
  133.2 1.1 fusion.84
  134.3 1.3 collective-permute-start.6
  135.6 4.0 %collective-permute-start.7 = (f32[4,1,128]{2,1,0:T(1,128)S(1)}, f32[4,1,128]{2,1,0:T(1,128)S(1)}, u32[]{:S(2)}, u32[]{:S(2)}) collective-permute-start(f32[4,1,128]{2,1,0:T(1,128)S(1)} %slice.259), channel_id=1, source_target_pairs={{16,0},{17,1},{18,2},{19,3},{20,4},{21,5},{22,6},{23,7},{24,8},{25... | collective-permute-start | bytes 6152 | tf_op jit(solution)/shard_map/ppermute | solution.py:22
  139.6 20.1 %all_gather.20 = f32[4,2,2048]{2,0,1:T(4,128)S(1)} all-gather(f32[4,2,128]{2,0,1:T(4,128)S(1)} %pad_maximum_fusion.16), channel_id=1, replica_groups=mesh['lat'=2,'lon'=16] {'lon'}, dimensions={2}, use_global_device_ids=true | all-gather | bytes 69632 | tf_op jit(solution)/shard_map/all_gather | solution.py:36
  159.7 1.1 copy.307
  160.8 0.7 gather_fusion.1
  161.5 0.1 copy.308
  161.7 0.5 collective-permute-start.5
  162.2 11.5 %collective-permute-done.4 = f32[4,256,1]{2,1,0:T(8,128)S(1)} collective-permute-done((f32[4,256,1]{2,1,0:T(8,128)}, f32[4,256,1]{2,1,0:T(8,128)S(1)}, u32[]{:S(2)}, u32[]{:S(2)}) %collective-permute-start.4) | collective-permute-done | bytes 4128 | tf_op jit(solution)/shard_map/ppermute | solution.py:20
  173.7 2.4 collective-permute-done.5
  176.2 1.7 fusion.41
  177.9 1.0 fusion.83
  179.0 1.3 collective-permute-start.10
  180.3 4.0 %collective-permute-start.11 = (f32[4,1,128]{2,1,0:T(1,128)S(1)}, f32[4,1,128]{2,1,0:T(1,128)S(1)}, u32[]{:S(2)}, u32[]{:S(2)}) collective-permute-start(f32[4,1,128]{2,1,0:T(1,128)S(1)} %get-tuple-element.29), channel_id=1, source_target_pairs={{16,0},{17,1},{18,2},{19,3},{20,4},{21,5},{22,6},{23,7},{24,8},{25... | collective-permute-start | bytes 6152 | tf_op jit(solution)/shard_map/ppermute | solution.py:22
  184.3 18.0 %all_gather.21 = f32[4,2,2048]{2,0,1:T(4,128)S(1)} all-gather(f32[4,2,128]{2,0,1:T(4,128)S(1)} %pad_maximum_fusion.17), channel_id=1, replica_groups=mesh['lat'=2,'lon'=16] {'lon'}, dimensions={2}, use_global_device_ids=true | all-gather | bytes 69632 | tf_op jit(solution)/shard_map/all_gather | solution.py:36
  202.2 2.3 copy.311
  204.6 2.3 gather_fusion.2
  206.9 0.1 copy.312
  207.1 0.5 collective-permute-start.9
  207.6 11.5 %collective-permute-done.8 = f32[4,256,1]{2,1,0:T(8,128)S(1)} collective-permute-done((f32[4,256,1]{2,1,0:T(8,128)}, f32[4,256,1]{2,1,0:T(8,128)S(1)}, u32[]{:S(2)}, u32[]{:S(2)}) %collective-permute-start.8) | collective-permute-done | bytes 4128 | tf_op jit(solution)/shard_map/ppermute | solution.py:20
  219.1 2.2 collective-permute-done.9
  221.3 0.5 fusion.35
  221.8 1.0 fusion.80
  222.9 1.3 collective-permute-start.14
  224.2 4.0 %collective-permute-start.15 = (f32[4,1,128]{2,1,0:T(1,128)S(1)}, f32[4,1,128]{2,1,0:T(1,128)S(1)}, u32[]{:S(2)}, u32[]{:S(2)}) collective-permute-start(f32[4,1,128]{2,1,0:T(1,128)S(1)} %get-tuple-element.23), channel_id=1, source_target_pairs={{16,0},{17,1},{18,2},{19,3},{20,4},{21,5},{22,6},{23,7},{24,8},{25... | collective-permute-start | bytes 6152 | tf_op jit(solution)/shard_map/ppermute | solution.py:22
  228.2 18.2 %all_gather.22 = f32[4,2,2048]{2,0,1:T(4,128)S(1)} all-gather(f32[4,2,128]{2,0,1:T(4,128)S(1)} %pad_maximum_fusion.18), channel_id=1, replica_groups=mesh['lat'=2,'lon'=16] {'lon'}, dimensions={2}, use_global_device_ids=true | all-gather | bytes 69632 | tf_op jit(solution)/shard_map/all_gather | solution.py:36
  246.4 2.3 copy.315
  248.8 2.3 gather_fusion.3
  251.1 0.1 copy.316
  251.2 0.5 collective-permute-start.13
  251.7 11.5 %collective-permute-done.12 = f32[4,256,1]{2,1,0:T(8,128)S(1)} collective-permute-done((f32[4,256,1]{2,1,0:T(8,128)}, f32[4,256,1]{2,1,0:T(8,128)S(1)}, u32[]{:S(2)}, u32[]{:S(2)}) %collective-permute-start.12) | collective-permute-done | bytes 4128 | tf_op jit(solution)/shard_map/ppermute | solution.py:20
  263.3 2.2 collective-permute-done.13
  265.5 0.5 fusion.29
  266.0 1.0 fusion.77
  267.1 1.3 collective-permute-start.18
  268.4 4.0 %collective-permute-start.19 = (f32[4,1,128]{2,1,0:T(1,128)S(1)}, f32[4,1,128]{2,1,0:T(1,128)S(1)}, u32[]{:S(2)}, u32[]{:S(2)}) collective-permute-start(f32[4,1,128]{2,1,0:T(1,128)S(1)} %get-tuple-element.17), channel_id=1, source_target_pairs={{16,0},{17,1},{18,2},{19,3},{20,4},{21,5},{22,6},{23,7},{24,8},{25... | collective-permute-start | bytes 6152 | tf_op jit(solution)/shard_map/ppermute | solution.py:22
  272.4 18.2 %all_gather.23 = f32[4,2,2048]{2,0,1:T(4,128)S(1)} all-gather(f32[4,2,128]{2,0,1:T(4,128)S(1)} %pad_maximum_fusion.19), channel_id=1, replica_groups=mesh['lat'=2,'lon'=16] {'lon'}, dimensions={2}, use_global_device_ids=true | all-gather | bytes 69632 | tf_op jit(solution)/shard_map/all_gather | solution.py:36
  290.6 2.3 copy.319
  292.9 2.3 gather_fusion.4
  295.4 0.5 collective-permute-start.17
  295.9 11.5 %collective-permute-done.16 = f32[4,256,1]{2,1,0:T(8,128)S(1)} collective-permute-done((f32[4,256,1]{2,1,0:T(8,128)}, f32[4,256,1]{2,1,0:T(8,128)S(1)}, u32[]{:S(2)}, u32[]{:S(2)}) %collective-permute-start.16) | collective-permute-done | bytes 4128 | tf_op jit(solution)/shard_map/ppermute | solution.py:20
  307.5 2.2 collective-permute-done.17
  309.7 1.3 fusion.23
  (62 shorter events, 0.9 us)
Async XLA Ops:
  7.2 8.7 %copy-start = (f32[4,256,128]{2,1,0:T(8,128)S(1)}, f32[4,256,128]{2,1,0:T(8,128)}, u32[]{:S(2)}) copy-start(f32[4,256,128]{2,1,0:T(8,128)} %param.8) | copy-start | bytes 1572868
  7.2 80.7 %all-gather.2.cloned.1.call-start = ((), (), s32[]{:S(2)}) async-start(), calls=%async_computation | async-start | bytes 2228224 | tf_op jit(solution)/shard_map/all_gather | solution.py:107
  8.0 35.2 %collective-permute-start.2 = (f32[4,1,128]{2,1,0:T(1,128)S(1)}, f32[4,1,128]{2,1,0:T(1,128)S(1)}, u32[]{:S(2)}, u32[]{:S(2)}) collective-permute-start(f32[4,1,128]{2,1,0:T(1,128)S(1)} %get-tuple-element.40), channel_id=1, source_target_pairs={{16,0},{17,1},{18,2},{19,3},{20,4},{21,5},{22,6},{23,7},{24,8},{25... | collective-permute-start | bytes 6152 | tf_op jit(solution)/shard_map/ppermute | solution.py:22
  9.3 33.9 %collective-permute-start.3 = (f32[4,1,128]{2,1,0:T(1,128)S(1)}, f32[4,1,128]{2,1,0:T(1,128)S(1)}, u32[]{:S(2)}, u32[]{:S(2)}) collective-permute-start(f32[4,1,128]{2,1,0:T(1,128)S(1)} %get-tuple-element.39), channel_id=1, source_target_pairs={{0,16},{1,17},{2,18},{3,19},{4,20},{5,21},{6,22},{7,23},{8,24},{9,... | collective-permute-start | bytes 6152 | tf_op jit(solution)/shard_map/ppermute | solution.py:20
  13.0 30.3 %collective-permute-start = (f32[4,256,1]{2,1,0:T(8,128)}, f32[4,256,1]{2,1,0:T(8,128)S(1)}, u32[]{:S(2)}, u32[]{:S(2)}) collective-permute-start(f32[4,256,1]{2,1,0:T(8,128)} %get-tuple-element.41), channel_id=1, source_target_pairs={{1,0},{2,1},{3,2},{4,3},{5,4},{6,5},{7,6},{8,7},{9,8},{10,9},{11,1... | collective-permute-start | bytes 12296 | tf_op jit(solution)/shard_map/ppermute | solution.py:22
  13.6 29.7 %collective-permute-start.1 = (f32[4,256,1]{2,1,0:T(8,128)}, f32[4,256,1]{2,1,0:T(8,128)}, u32[]{:S(2)}, u32[]{:S(2)}) collective-permute-start(f32[4,256,1]{2,1,0:T(8,128)} %get-tuple-element.42), channel_id=1, source_target_pairs={{0,1},{1,2},{2,3},{3,4},{4,5},{5,6},{6,7},{7,8},{8,9},{9,10},{10,1... | collective-permute-start | bytes 12296 | tf_op jit(solution)/shard_map/ppermute | solution.py:20
  43.3 0.8 copy-start.3
  44.1 3.0 copy-start.4
  87.8 22.8 %copy-start.5 = (f32[256,2048]{1,0:T(8,128)S(1)}, f32[256,2048]{1,0:T(8,128)}, u32[]{:S(2)}) copy-start(f32[256,2048]{1,0:T(8,128)} %all-gather.2.cloned.1.call-done) | copy-start | bytes 6291460
  132.0 7.5 %copy-start.1 = (f32[4,256,128]{2,1,0:T(8,128)}, f32[4,256,128]{2,1,0:T(8,128)S(1)}, u32[]{:S(2)}) copy-start(f32[4,256,128]{2,1,0:T(8,128)S(1)} %pad_maximum_fusion.14) | copy-start | bytes 1572868
  133.2 43.0 %copy-start.2 = (f32[4,256,128]{2,1,0:T(8,128)S(1)}, f32[4,256,128]{2,1,0:T(8,128)}, u32[]{:S(2)}) copy-start(f32[4,256,128]{2,1,0:T(8,128)} %param.11) | copy-start | bytes 1572868
  134.3 27.9 %collective-permute-start.6 = (f32[4,1,128]{2,1,0:T(1,128)S(1)}, f32[4,1,128]{2,1,0:T(1,128)S(1)}, u32[]{:S(2)}, u32[]{:S(2)}) collective-permute-start(f32[4,1,128]{2,1,0:T(1,128)S(1)} %slice.260), channel_id=1, source_target_pairs={{0,16},{1,17},{2,18},{3,19},{4,20},{5,21},{6,22},{7,23},{8,24},{9,... | collective-permute-start | bytes 6152 | tf_op jit(solution)/shard_map/ppermute | solution.py:20
  135.6 26.6 %collective-permute-start.7 = (f32[4,1,128]{2,1,0:T(1,128)S(1)}, f32[4,1,128]{2,1,0:T(1,128)S(1)}, u32[]{:S(2)}, u32[]{:S(2)}) collective-permute-start(f32[4,1,128]{2,1,0:T(1,128)S(1)} %slice.259), channel_id=1, source_target_pairs={{16,0},{17,1},{18,2},{19,3},{20,4},{21,5},{22,6},{23,7},{24,8},{25... | collective-permute-start | bytes 6152 | tf_op jit(solution)/shard_map/ppermute | solution.py:22
  161.6 12.1 %collective-permute-start.4 = (f32[4,256,1]{2,1,0:T(8,128)}, f32[4,256,1]{2,1,0:T(8,128)S(1)}, u32[]{:S(2)}, u32[]{:S(2)}) collective-permute-start(f32[4,256,1]{2,1,0:T(8,128)} %get-tuple-element.35), channel_id=1, source_target_pairs={{0,1},{1,2},{2,3},{3,4},{4,5},{5,6},{6,7},{7,8},{8,9},{9,10},{10,1... | collective-permute-start | bytes 12296 | tf_op jit(solution)/shard_map/ppermute | solution.py:20
  161.7 14.5 %collective-permute-start.5 = (f32[4,256,1]{2,1,0:T(8,128)}, f32[4,256,1]{2,1,0:T(8,128)S(1)}, u32[]{:S(2)}, u32[]{:S(2)}) collective-permute-start(f32[4,256,1]{2,1,0:T(8,128)} %get-tuple-element.36), channel_id=1, source_target_pairs={{1,0},{2,1},{3,2},{4,3},{5,4},{6,5},{7,6},{8,7},{9,8},{10,9},{11,1... | collective-permute-start | bytes 12296 | tf_op jit(solution)/shard_map/ppermute | solution.py:22
  179.0 28.6 %collective-permute-start.10 = (f32[4,1,128]{2,1,0:T(1,128)S(1)}, f32[4,1,128]{2,1,0:T(1,128)S(1)}, u32[]{:S(2)}, u32[]{:S(2)}) collective-permute-start(f32[4,1,128]{2,1,0:T(1,128)S(1)} %get-tuple-element.30), channel_id=1, source_target_pairs={{0,16},{1,17},{2,18},{3,19},{4,20},{5,21},{6,22},{7,23},{8,24},{9,... | collective-permute-start | bytes 6152 | tf_op jit(solution)/shard_map/ppermute | solution.py:20
  180.3 27.3 %collective-permute-start.11 = (f32[4,1,128]{2,1,0:T(1,128)S(1)}, f32[4,1,128]{2,1,0:T(1,128)S(1)}, u32[]{:S(2)}, u32[]{:S(2)}) collective-permute-start(f32[4,1,128]{2,1,0:T(1,128)S(1)} %get-tuple-element.29), channel_id=1, source_target_pairs={{16,0},{17,1},{18,2},{19,3},{20,4},{21,5},{22,6},{23,7},{24,8},{25... | collective-permute-start | bytes 6152 | tf_op jit(solution)/shard_map/ppermute | solution.py:22
  207.0 12.1 %collective-permute-start.8 = (f32[4,256,1]{2,1,0:T(8,128)}, f32[4,256,1]{2,1,0:T(8,128)S(1)}, u32[]{:S(2)}, u32[]{:S(2)}) collective-permute-start(f32[4,256,1]{2,1,0:T(8,128)} %get-tuple-element.31), channel_id=1, source_target_pairs={{0,1},{1,2},{2,3},{3,4},{4,5},{5,6},{6,7},{7,8},{8,9},{9,10},{10,1... | collective-permute-start | bytes 12296 | tf_op jit(solution)/shard_map/ppermute | solution.py:20
  207.1 14.3 %collective-permute-start.9 = (f32[4,256,1]{2,1,0:T(8,128)S(1)}, f32[4,256,1]{2,1,0:T(8,128)S(1)}, u32[]{:S(2)}, u32[]{:S(2)}) collective-permute-start(f32[4,256,1]{2,1,0:T(8,128)S(1)} %get-tuple-element.32), channel_id=1, source_target_pairs={{1,0},{2,1},{3,2},{4,3},{5,4},{6,5},{7,6},{8,7},{9,8},{10,9},{11,1... | collective-permute-start | bytes 12296 | tf_op jit(solution)/shard_map/ppermute | solution.py:22
  222.9 28.8 %collective-permute-start.14 = (f32[4,1,128]{2,1,0:T(1,128)S(1)}, f32[4,1,128]{2,1,0:T(1,128)S(1)}, u32[]{:S(2)}, u32[]{:S(2)}) collective-permute-start(f32[4,1,128]{2,1,0:T(1,128)S(1)} %get-tuple-element.24), channel_id=1, source_target_pairs={{0,16},{1,17},{2,18},{3,19},{4,20},{5,21},{6,22},{7,23},{8,24},{9,... | collective-permute-start | bytes 6152 | tf_op jit(solution)/shard_map/ppermute | solution.py:20
  224.2 27.5 %collective-permute-start.15 = (f32[4,1,128]{2,1,0:T(1,128)S(1)}, f32[4,1,128]{2,1,0:T(1,128)S(1)}, u32[]{:S(2)}, u32[]{:S(2)}) collective-permute-start(f32[4,1,128]{2,1,0:T(1,128)S(1)} %get-tuple-element.23), channel_id=1, source_target_pairs={{16,0},{17,1},{18,2},{19,3},{20,4},{21,5},{22,6},{23,7},{24,8},{25... | collective-permute-start | bytes 6152 | tf_op jit(solution)/shard_map/ppermute | solution.py:22
  251.2 12.1 %collective-permute-start.12 = (f32[4,256,1]{2,1,0:T(8,128)}, f32[4,256,1]{2,1,0:T(8,128)S(1)}, u32[]{:S(2)}, u32[]{:S(2)}) collective-permute-start(f32[4,256,1]{2,1,0:T(8,128)} %get-tuple-element.25), channel_id=1, source_target_pairs={{0,1},{1,2},{2,3},{3,4},{4,5},{5,6},{6,7},{7,8},{8,9},{9,10},{10,1... | collective-permute-start | bytes 12296 | tf_op jit(solution)/shard_map/ppermute | solution.py:20
  251.2 14.3 %collective-permute-start.13 = (f32[4,256,1]{2,1,0:T(8,128)S(1)}, f32[4,256,1]{2,1,0:T(8,128)S(1)}, u32[]{:S(2)}, u32[]{:S(2)}) collective-permute-start(f32[4,256,1]{2,1,0:T(8,128)S(1)} %get-tuple-element.26), channel_id=1, source_target_pairs={{1,0},{2,1},{3,2},{4,3},{5,4},{6,5},{7,6},{8,7},{9,8},{10,9},{11,1... | collective-permute-start | bytes 12296 | tf_op jit(solution)/shard_map/ppermute | solution.py:22
  267.1 28.8 %collective-permute-start.18 = (f32[4,1,128]{2,1,0:T(1,128)S(1)}, f32[4,1,128]{2,1,0:T(1,128)S(1)}, u32[]{:S(2)}, u32[]{:S(2)}) collective-permute-start(f32[4,1,128]{2,1,0:T(1,128)S(1)} %get-tuple-element.18), channel_id=1, source_target_pairs={{0,16},{1,17},{2,18},{3,19},{4,20},{5,21},{6,22},{7,23},{8,24},{9,... | collective-permute-start | bytes 6152 | tf_op jit(solution)/shard_map/ppermute | solution.py:20
  268.4 27.5 %collective-permute-start.19 = (f32[4,1,128]{2,1,0:T(1,128)S(1)}, f32[4,1,128]{2,1,0:T(1,128)S(1)}, u32[]{:S(2)}, u32[]{:S(2)}) collective-permute-start(f32[4,1,128]{2,1,0:T(1,128)S(1)} %get-tuple-element.17), channel_id=1, source_target_pairs={{16,0},{17,1},{18,2},{19,3},{20,4},{21,5},{22,6},{23,7},{24,8},{25... | collective-permute-start | bytes 6152 | tf_op jit(solution)/shard_map/ppermute | solution.py:22
  295.4 12.1 %collective-permute-start.16 = (f32[4,256,1]{2,1,0:T(8,128)}, f32[4,256,1]{2,1,0:T(8,128)S(1)}, u32[]{:S(2)}, u32[]{:S(2)}) collective-permute-start(f32[4,256,1]{2,1,0:T(8,128)} %get-tuple-element.19), channel_id=1, source_target_pairs={{0,1},{1,2},{2,3},{3,4},{4,5},{5,6},{6,7},{7,8},{8,9},{9,10},{10,1... | collective-permute-start | bytes 12296 | tf_op jit(solution)/shard_map/ppermute | solution.py:20
  295.4 14.3 %collective-permute-start.17 = (f32[4,256,1]{2,1,0:T(8,128)S(1)}, f32[4,256,1]{2,1,0:T(8,128)S(1)}, u32[]{:S(2)}, u32[]{:S(2)}) collective-permute-start(f32[4,256,1]{2,1,0:T(8,128)S(1)} %get-tuple-element.20), channel_id=1, source_target_pairs={{1,0},{2,1},{3,2},{4,3},{5,4},{6,5},{7,6},{8,7},{9,8},{10,9},{11,1... | collective-permute-start | bytes 12296 | tf_op jit(solution)/shard_map/ppermute | solution.py:22
Sparse Core Ops, SparseCore 0:
  47.2 40.5 all-gather.1
where the time goes:
time: 318 us
  blocking collectives  98.1 us (31%)
  waiting for transfers between devices  95.9 us (30%)
  matrix products  44 us (14%)
  starting transfers between devices  28.8 us (9%)
  local copies, waits for them, and re-layouts  28.6 us (9%)
  between operations  14.5 us (5%)
  other arithmetic  8 us (3%)
    all_gather x5, blocking collectives, neighbours(): whole_rows = lax.all_gather(edge_rows, 'lon', axis=2, tiled=True)  98.1 us
    ppermute x10, waiting for transfers between devices, padded(): lax.ppermute(tail, axis, [(i, (i + 1) % count) for i in range(ends)])  46.2 us
    all_gather x1, waiting for transfers between devices, polar_filter(): lax.all_gather(flat, 'lon', axis=1, tiled=True)  40.6 us
    dot_general x1, matrix products, project(): jnp.dot(rows, cosine, precision=lax.Precision.HIGHEST, preferred_element_...  21.2 us
    ppermute x10, starting transfers between devices, padded(): lax.ppermute(head, axis, [((i + 1) % count, i) for i in range(ends)])  19.9 us
    dot_general x1, matrix products, project(): jnp.dot(rows, sine, precision=lax.Precision.HIGHEST, preferred_element_ty...  19.7 us
    all_gather x5, local copies, waits for them, and re-layouts, neighbours(): whole_rows = lax.all_gather(edge_rows, 'lon', axis=2, tiled=True)  9.14 us
    ppermute x10, waiting for transfers between devices, padded(): lax.ppermute(head, axis, [((i + 1) % count, i) for i in range(ends)])  9.13 us
  transfers between devices with their start and end apart: 21, of which 9 were waited for; matrix products, arithmetic and copies ran while one was open for 7% of the time, Pallas kernels for 0%

commit v1 on v0

--- a/solution.py
+++ b/solution.py
@@ -1,12 +1,32 @@
+import functools
 import math
 import jax
 import jax.numpy as jnp
 from jax import lax
 from jax.sharding import PartitionSpec as P
+from jax.lax import axis_index, axis_size, ppermute
 
 KMAX = 512
 SWEEPS = 4
 COURANT = 0.4
+
+
+def register_the_cells(block_in, shard_axis):
+    cores_n = axis_size(shard_axis)
+    items = tuple(((pp, (pp + 1) % cores_n) for pp in range(cores_n)))
+
+    def mark_members_all(x_now):
+        if len(x_now) == cores_n:
+            return x_now
+        small = mark_members_all([ppermute(x_now[0], axis_name=shard_axis, perm=items), *x_now])
+        return small
+
+    front = jnp.concatenate(mark_members_all([block_in]), axis=2)
+    carry_in = jnp.roll(front, (axis_index(shard_axis) + 1) * block_in.shape[2], axis=2)
+    return carry_in
+
+
+follow_bars = functools.partial(register_the_cells, shard_axis="lon")
 
 
 def padded(cells, sides, width, closed):
@@ -33,7 +53,7 @@
     lat_padded = padded(field, (("lat", 1),), 1, False)
     edge_rows = jnp.stack([field[:, 0, :], field[:, -1, :]], axis=1)
     own_partner = lax.dynamic_slice_in_dim(partner, lon_index * width, width)
-    whole_rows = lax.all_gather(edge_rows, "lon", axis=2, tiled=True)
+    whole_rows = follow_bars(edge_rows)
     across = jnp.take(whole_rows, own_partner, axis=2)
     lat_index = lax.axis_index("lat")
     last_band = lax.axis_size("lat") - 1

time: 318 us -> 580 us (1.82); the launches traced: 318 us -> 572 us
  waiting for transfers between devices: 95.9 us -> 407 us
  blocking collectives: 98.1 us -> 0 us
  starting transfers between devices: 28.8 us -> 62.5 us
    ppermute x0 -> x75, waiting for transfers between devices: none -> 362 us  [mark_members_all(): ppermute(x_now[0], axis_name=shard_axis, perm=items)]
    all_gather x5 -> x0, blocking collectives: 98.1 us -> none  [neighbours(): whole_rows = lax.all_gather(edge_rows, 'lon', axis=2, tiled=True)]
    ppermute x10, waiting for transfers between devices: 46.2 us -> 0.04 us  [padded(): lax.ppermute(tail, axis, [(i, (i + 1) % count) for i in range(ends)])]
    ppermute x10, starting transfers between devices: 19.9 us -> 43.5 us  [padded(): lax.ppermute(head, axis, [((i + 1) % count, i) for i in range(ends)])]
    ppermute x0 -> x75, starting transfers between devices: none -> 12.3 us  [mark_members_all(): ppermute(x_now[0], axis_name=shard_axis, perm=items)]
    unnamed x12 -> x96, local copies, waits for them, and re-layouts: 0.8 us -> 12.2 us
    all_gather x5 -> x0, local copies, waits for them, and re-layouts: 9.14 us -> none  [neighbours(): whole_rows = lax.all_gather(edge_rows, 'lon', axis=2, tiled=True)]
    ppermute x10, waiting for transfers between devices: 9.13 us -> 1.76 us  [padded(): lax.ppermute(head, axis, [((i + 1) % count, i) for i in range(ends)])]
  transfers between devices with their start and end apart: 21 -> 96, of which waited for: 9 -> 75; matrix products, arithmetic and copies ran while one was open for 7% -> 5% of each run, Pallas kernels for 0% -> 0%
where the time goes in v1:
time: 580 us; the launch traced here: 572 us
  waiting for transfers between devices  407 us (70%)
  starting transfers between devices  62.5 us (11%)
  matrix products  44 us (8%)
  local copies, waits for them, and re-layouts  31.1 us (5%)
  between operations  15.3 us (3%)
  other arithmetic  12 us (2%)
    ppermute x75, waiting for transfers between devices, mark_members_all(): ppermute(x_now[0], axis_name=shard_axis, perm=items)  362 us
    ppermute x10, starting transfers between devices, padded(): lax.ppermute(head, axis, [((i + 1) % count, i) for i in range(ends)])  43.5 us
    all_gather x1, waiting for transfers between devices, polar_filter(): lax.all_gather(flat, 'lon', axis=1, tiled=True)  43.3 us
    dot_general x1, matrix products, project(): jnp.dot(rows, cosine, precision=lax.Precision.HIGHEST, preferred_element_...  21.2 us
    dot_general x1, matrix products, project(): jnp.dot(rows, sine, precision=lax.Precision.HIGHEST, preferred_element_ty...  19.7 us
    ppermute x75, starting transfers between devices, mark_members_all(): ppermute(x_now[0], axis_name=shard_axis, perm=items)  12.3 us
    unnamed x96, local copies, waits for them, and re-layouts  12.2 us
  transfers between devices with their start and end apart: 96, of which 75 were waited for; matrix products, arithmetic and copies ran while one was open for 5% of the time, Pallas kernels for 0%

profile of v1, /device:TPU:3, one launch (start us, length us, event | category | flops | bytes accessed | tf_op | source)
XLA Modules:
  0.0 571.6 jit_solution(9593816063227980935)
XLA Ops:
  20.9 5.7 %collective-permute-done.5 = f32[4,2,128]{2,0,1:T(4,128)S(1)} collective-permute-done((f32[4,2,128]{2,0,1:T(4,128)S(1)}, f32[4,2,128]{2,0,1:T(4,128)S(1)}, u32[]{:S(2)}, u32[]{:S(2)}) %collective-permute-start.5) | collective-permute-done | bytes 4128 | tf_op jit(solution)/shard_map/ppermute | solution.py:21
  26.6 5.7 %collective-permute-done.6 = f32[4,2,128]{2,0,1:T(4,128)S(1)} collective-permute-done((f32[4,2,128]{2,0,1:T(4,128)S(1)}, f32[4,2,128]{2,0,1:T(4,128)S(1)}, u32[]{:S(2)}, u32[]{:S(2)}) %collective-permute-start.6) | collective-permute-done | bytes 4128 | tf_op jit(solution)/shard_map/ppermute | solution.py:21
  32.3 5.7 %collective-permute-done.7 = f32[4,2,128]{2,0,1:T(4,128)S(1)} collective-permute-done((f32[4,2,128]{2,0,1:T(4,128)S(1)}, f32[4,2,128]{2,0,1:T(4,128)S(1)}, u32[]{:S(2)}, u32[]{:S(2)}) %collective-permute-start.7) | collective-permute-done | bytes 4128 | tf_op jit(solution)/shard_map/ppermute | solution.py:21
  38.1 5.7 %collective-permute-done.8 = f32[4,2,128]{2,0,1:T(4,128)S(1)} collective-permute-done((f32[4,2,128]{2,0,1:T(4,128)S(1)}, f32[4,2,128]{2,0,1:T(4,128)S(1)}, u32[]{:S(2)}, u32[]{:S(2)}) %collective-permute-start.8) | collective-permute-done | bytes 4128 | tf_op jit(solution)/shard_map/ppermute | solution.py:21
  43.8 5.7 %collective-permute-done.9 = f32[4,2,128]{2,0,1:T(4,128)S(1)} collective-permute-done((f32[4,2,128]{2,0,1:T(4,128)S(1)}, f32[4,2,128]{2,0,1:T(4,128)S(1)}, u32[]{:S(2)}, u32[]{:S(2)}) %collective-permute-start.9) | collective-permute-done | bytes 4128 | tf_op jit(solution)/shard_map/ppermute | solution.py:21
  49.5 5.7 %collective-permute-done.10 = f32[4,2,128]{2,0,1:T(4,128)S(1)} collective-permute-done((f32[4,2,128]{2,0,1:T(4,128)S(1)}, f32[4,2,128]{2,0,1:T(4,128)S(1)}, u32[]{:S(2)}, u32[]{:S(2)}) %collective-permute-start.10) | collective-permute-done | bytes 4128 | tf_op jit(solution)/shard_map/ppermute | solution.py:21
  55.2 5.7 %collective-permute-done.11 = f32[4,2,128]{2,0,1:T(4,128)S(1)} collective-permute-done((f32[4,2,128]{2,0,1:T(4,128)S(1)}, f32[4,2,128]{2,0,1:T(4,128)S(1)}, u32[]{:S(2)}, u32[]{:S(2)}) %collective-permute-start.11) | collective-permute-done | bytes 4128 | tf_op jit(solution)/shard_map/ppermute | solution.py:21
  69.1 5.1 collective-permute-start
  75.2 5.4 collective-permute-done.14
  83.8 7.0 %collective-permute-done.15 = f32[4,2,128]{2,0,1:T(4,128)S(1)} collective-permute-done((f32[4,2,128]{2,0,1:T(4,128)S(1)}, f32[4,2,128]{2,0,1:T(4,128)S(1)}, u32[]{:S(2)}, u32[]{:S(2)}) %collective-permute-start.15) | collective-permute-done | bytes 4128 | tf_op jit(solution)/shard_map/ppermute | solution.py:21
  91.4 5.7 collective-permute-done.16
  103.3 43.3 %all-gather.2.cloned.1.call-done = f32[256,2048]{1,0:T(8,128)} async-done(((f32[256,128]{1,0:T(8,128)}), f32[256,2048]{1,0:T(8,128)}) %all-gather.2.cloned.1.call-update) | async-done | bytes 2097168 | tf_op jit(solution)/shard_map/all_gather | solution.py:127
  146.6 21.2 %fusion.12 = f32[256,512]{1,0:T(8,128)S(1)} fusion(f32[256,2048]{1,0:T(8,128)} %all-gather.2.cloned.1.call-done, f32[512]{0:T(512)S(1)} %select_multiply_fusion, s32[256]{0:T(256)S(1)} %le.23), kind=kOutput, calls=%fused_computation.18 | convolution fusion | flops 3236298752 | bytes 2624512 | tf_op jit(solution)/shard_map/dot_general | solution.py:79
  169.4 19.7 %fusion.15 = f32[256,512]{1,0:T(8,128)S(1)} fusion(f32[256,2048]{1,0:T(8,128)S(1)} %copy-done.7, f32[512]{0:T(512)S(1)} %select_multiply_fusion, s32[256]{0:T(256)S(1)} %le.23), kind=kOutput, calls=%fused_computation.19 | convolution fusion | flops 3236298752 | bytes 2624512 | tf_op jit(solution)/shard_map/dot_general | solution.py:82
  197.8 5.3 collective-permute-done.23
  203.1 5.7 %collective-permute-done.24 = f32[4,2,128]{2,0,1:T(4,128)S(1)} collective-permute-done((f32[4,2,128]{2,0,1:T(4,128)S(1)}, f32[4,2,128]{2,0,1:T(4,128)S(1)}, u32[]{:S(2)}, u32[]{:S(2)}) %collective-permute-start.24) | collective-permute-done | bytes 4128 | tf_op jit(solution)/shard_map/ppermute | solution.py:21
  208.9 5.7 %collective-permute-done.25 = f32[4,2,128]{2,0,1:T(4,128)S(1)} collective-permute-done((f32[4,2,128]{2,0,1:T(4,128)S(1)}, f32[4,2,128]{2,0,1:T(4,128)S(1)}, u32[]{:S(2)}, u32[]{:S(2)}) %collective-permute-start.25) | collective-permute-done | bytes 4128 | tf_op jit(solution)/shard_map/ppermute | solution.py:21
  214.6 5.7 %collective-permute-done.26 = f32[4,2,128]{2,0,1:T(4,128)S(1)} collective-permute-done((f32[4,2,128]{2,0,1:T(4,128)S(1)}, f32[4,2,128]{2,0,1:T(4,128)S(1)}, u32[]{:S(2)}, u32[]{:S(2)}) %collective-permute-start.26) | collective-permute-done | bytes 4128 | tf_op jit(solution)/shard_map/ppermute | solution.py:21
  220.3 5.7 %collective-permute-done.27 = f32[4,2,128]{2,0,1:T(4,128)S(1)} collective-permute-done((f32[4,2,128]{2,0,1:T(4,128)S(1)}, f32[4,2,128]{2,0,1:T(4,128)S(1)}, u32[]{:S(2)}, u32[]{:S(2)}) %collective-permute-start.27) | collective-permute-done | bytes 4128 | tf_op jit(solution)/shard_map/ppermute | solution.py:21
  226.1 5.7 %collective-permute-done.28 = f32[4,2,128]{2,0,1:T(4,128)S(1)} collective-permute-done((f32[4,2,128]{2,0,1:T(4,128)S(1)}, f32[4,2,128]{2,0,1:T(4,128)S(1)}, u32[]{:S(2)}, u32[]{:S(2)}) %collective-permute-start.28) | collective-permute-done | bytes 4128 | tf_op jit(solution)/shard_map/ppermute | solution.py:21
  231.8 5.7 %collective-permute-done.29 = f32[4,2,128]{2,0,1:T(4,128)S(1)} collective-permute-done((f32[4,2,128]{2,0,1:T(4,128)S(1)}, f32[4,2,128]{2,0,1:T(4,128)S(1)}, u32[]{:S(2)}, u32[]{:S(2)}) %collective-permute-start.29) | collective-permute-done | bytes 4128 | tf_op jit(solution)/shard_map/ppermute | solution.py:21
  237.5 5.7 %collective-permute-done.30 = f32[4,2,128]{2,0,1:T(4,128)S(1)} collective-permute-done((f32[4,2,128]{2,0,1:T(4,128)S(1)}, f32[4,2,128]{2,0,1:T(4,128)S(1)}, u32[]{:S(2)}, u32[]{:S(2)}) %collective-permute-start.30) | collective-permute-done | bytes 4128 | tf_op jit(solution)/shard_map/ppermute | solution.py:21
  243.3 5.7 %collective-permute-done.31 = f32[4,2,128]{2,0,1:T(4,128)S(1)} collective-permute-done((f32[4,2,128]{2,0,1:T(4,128)S(1)}, f32[4,2,128]{2,0,1:T(4,128)S(1)}, u32[]{:S(2)}, u32[]{:S(2)}) %collective-permute-start.31) | collective-permute-done | bytes 4128 | tf_op jit(solution)/shard_map/ppermute | solution.py:21
  254.8 5.9 %collective-permute-done.33 = f32[4,2,128]{2,0,1:T(4,128)S(1)} collective-permute-done((f32[4,2,128]{2,0,1:T(4,128)S(1)}, f32[4,2,128]{2,0,1:T(4,128)S(1)}, u32[]{:S(2)}, u32[]{:S(2)}) %collective-permute-start.33) | collective-permute-done | bytes 4128 | tf_op jit(solution)/shard_map/ppermute | solution.py:21
  267.4 5.2 collective-permute-start.20
  278.7 8.3 %collective-permute-done.40 = f32[4,2,128]{2,0,1:T(4,128)S(1)} collective-permute-done((f32[4,2,128]{2,0,1:T(4,128)S(1)}, f32[4,2,128]{2,0,1:T(4,128)S(1)}, u32[]{:S(2)}, u32[]{:S(2)}) %collective-permute-start.40) | collective-permute-done | bytes 4128 | tf_op jit(solution)/shard_map/ppermute | solution.py:21
  287.0 5.7 %collective-permute-done.41 = f32[4,2,128]{2,0,1:T(4,128)S(1)} collective-permute-done((f32[4,2,128]{2,0,1:T(4,128)S(1)}, f32[4,2,128]{2,0,1:T(4,128)S(1)}, u32[]{:S(2)}, u32[]{:S(2)}) %collective-permute-start.41) | collective-permute-done | bytes 4128 | tf_op jit(solution)/shard_map/ppermute | solution.py:21
  292.7 5.7 %collective-permute-done.42 = f32[4,2,128]{2,0,1:T(4,128)S(1)} collective-permute-done((f32[4,2,128]{2,0,1:T(4,128)S(1)}, f32[4,2,128]{2,0,1:T(4,128)S(1)}, u32[]{:S(2)}, u32[]{:S(2)}) %collective-permute-start.42) | collective-permute-done | bytes 4128 | tf_op jit(solution)/shard_map/ppermute | solution.py:21
  298.4 5.7 %collective-permute-done.43 = f32[4,2,128]{2,0,1:T(4,128)S(1)} collective-permute-done((f32[4,2,128]{2,0,1:T(4,128)S(1)}, f32[4,2,128]{2,0,1:T(4,128)S(1)}, u32[]{:S(2)}, u32[]{:S(2)}) %collective-permute-start.43) | collective-permute-done | bytes 4128 | tf_op jit(solution)/shard_map/ppermute | solution.py:21
  304.1 5.7 %collective-permute-done.44 = f32[4,2,128]{2,0,1:T(4,128)S(1)} collective-permute-done((f32[4,2,128]{2,0,1:T(4,128)S(1)}, f32[4,2,128]{2,0,1:T(4,128)S(1)}, u32[]{:S(2)}, u32[]{:S(2)}) %collective-permute-start.44) | collective-permute-done | bytes 4128 | tf_op jit(solution)/shard_map/ppermute | solution.py:21
  309.9 5.7 %collective-permute-done.45 = f32[4,2,128]{2,0,1:T(4,128)S(1)} collective-permute-done((f32[4,2,128]{2,0,1:T(4,128)S(1)}, f32[4,2,128]{2,0,1:T(4,128)S(1)}, u32[]{:S(2)}, u32[]{:S(2)}) %collective-permute-start.45) | collective-permute-done | bytes 4128 | tf_op jit(solution)/shard_map/ppermute | solution.py:21
  315.6 5.7 %collective-permute-done.46 = f32[4,2,128]{2,0,1:T(4,128)S(1)} collective-permute-done((f32[4,2,128]{2,0,1:T(4,128)S(1)}, f32[4,2,128]{2,0,1:T(4,128)S(1)}, u32[]{:S(2)}, u32[]{:S(2)}) %collective-permute-start.46) | collective-permute-done | bytes 4128 | tf_op jit(solution)/shard_map/ppermute | solution.py:21
  321.3 5.7 %collective-permute-done.47 = f32[4,2,128]{2,0,1:T(4,128)S(1)} collective-permute-done((f32[4,2,128]{2,0,1:T(4,128)S(1)}, f32[4,2,128]{2,0,1:T(4,128)S(1)}, u32[]{:S(2)}, u32[]{:S(2)}) %collective-permute-start.47) | collective-permute-done | bytes 4128 | tf_op jit(solution)/shard_map/ppermute | solution.py:21
  327.1 5.7 %collective-permute-done.48 = f32[4,2,128]{2,0,1:T(4,128)S(1)} collective-permute-done((f32[4,2,128]{2,0,1:T(4,128)S(1)}, f32[4,2,128]{2,0,1:T(4,128)S(1)}, u32[]{:S(2)}, u32[]{:S(2)}) %collective-permute-start.48) | collective-permute-done | bytes 4128 | tf_op jit(solution)/shard_map/ppermute | solution.py:21
  332.8 5.7 %collective-permute-done.49 = f32[4,2,128]{2,0,1:T(4,128)S(1)} collective-permute-done((f32[4,2,128]{2,0,1:T(4,128)S(1)}, f32[4,2,128]{2,0,1:T(4,128)S(1)}, u32[]{:S(2)}, u32[]{:S(2)}) %collective-permute-start.49) | collective-permute-done | bytes 4128 | tf_op jit(solution)/shard_map/ppermute | solution.py:21
  338.5 5.7 %collective-permute-done.50 = f32[4,2,128]{2,0,1:T(4,128)S(1)} collective-permute-done((f32[4,2,128]{2,0,1:T(4,128)S(1)}, f32[4,2,128]{2,0,1:T(4,128)S(1)}, u32[]{:S(2)}, u32[]{:S(2)}) %collective-permute-start.50) | collective-permute-done | bytes 4128 | tf_op jit(solution)/shard_map/ppermute | solution.py:21
  344.3 5.7 %collective-permute-done.51 = f32[4,2,128]{2,0,1:T(4,128)S(1)} collective-permute-done((f32[4,2,128]{2,0,1:T(4,128)S(1)}, f32[4,2,128]{2,0,1:T(4,128)S(1)}, u32[]{:S(2)}, u32[]{:S(2)}) %collective-permute-start.51) | collective-permute-done | bytes 4128 | tf_op jit(solution)/shard_map/ppermute | solution.py:21
  361.8 5.2 collective-permute-start.39
  375.1 6.6 %collective-permute-done.59 = f32[4,2,128]{2,0,1:T(4,128)S(1)} collective-permute-done((f32[4,2,128]{2,0,1:T(4,128)S(1)}, f32[4,2,128]{2,0,1:T(4,128)S(1)}, u32[]{:S(2)}, u32[]{:S(2)}) %collective-permute-start.59) | collective-permute-done | bytes 4128 | tf_op jit(solution)/shard_map/ppermute | solution.py:21
  381.7 5.7 %collective-permute-done.60 = f32[4,2,128]{2,0,1:T(4,128)S(1)} collective-permute-done((f32[4,2,128]{2,0,1:T(4,128)S(1)}, f32[4,2,128]{2,0,1:T(4,128)S(1)}, u32[]{:S(2)}, u32[]{:S(2)}) %collective-permute-start.60) | collective-permute-done | bytes 4128 | tf_op jit(solution)/shard_map/ppermute | solution.py:21
  387.4 5.7 %collective-permute-done.61 = f32[4,2,128]{2,0,1:T(4,128)S(1)} collective-permute-done((f32[4,2,128]{2,0,1:T(4,128)S(1)}, f32[4,2,128]{2,0,1:T(4,128)S(1)}, u32[]{:S(2)}, u32[]{:S(2)}) %collective-permute-start.61) | collective-permute-done | bytes 4128 | tf_op jit(solution)/shard_map/ppermute | solution.py:21
  393.1 5.7 %collective-permute-done.62 = f32[4,2,128]{2,0,1:T(4,128)S(1)} collective-permute-done((f32[4,2,128]{2,0,1:T(4,128)S(1)}, f32[4,2,128]{2,0,1:T(4,128)S(1)}, u32[]{:S(2)}, u32[]{:S(2)}) %collective-permute-start.62) | collective-permute-done | bytes 4128 | tf_op jit(solution)/shard_map/ppermute | solution.py:21
  398.8 5.7 %collective-permute-done.63 = f32[4,2,128]{2,0,1:T(4,128)S(1)} collective-permute-done((f32[4,2,128]{2,0,1:T(4,128)S(1)}, f32[4,2,128]{2,0,1:T(4,128)S(1)}, u32[]{:S(2)}, u32[]{:S(2)}) %collective-permute-start.63) | collective-permute-done | bytes 4128 | tf_op jit(solution)/shard_map/ppermute | solution.py:21
  404.6 5.7 %collective-permute-done.64 = f32[4,2,128]{2,0,1:T(4,128)S(1)} collective-permute-done((f32[4,2,128]{2,0,1:T(4,128)S(1)}, f32[4,2,128]{2,0,1:T(4,128)S(1)}, u32[]{:S(2)}, u32[]{:S(2)}) %collective-permute-start.64) | collective-permute-done | bytes 4128 | tf_op jit(solution)/shard_map/ppermute | solution.py:21
  410.3 5.7 %collective-permute-done.65 = f32[4,2,128]{2,0,1:T(4,128)S(1)} collective-permute-done((f32[4,2,128]{2,0,1:T(4,128)S(1)}, f32[4,2,128]{2,0,1:T(4,128)S(1)}, u32[]{:S(2)}, u32[]{:S(2)}) %collective-permute-start.65) | collective-permute-done | bytes 4128 | tf_op jit(solution)/shard_map/ppermute | solution.py:21
  416.0 5.7 %collective-permute-done.66 = f32[4,2,128]{2,0,1:T(4,128)S(1)} collective-permute-done((f32[4,2,128]{2,0,1:T(4,128)S(1)}, f32[4,2,128]{2,0,1:T(4,128)S(1)}, u32[]{:S(2)}, u32[]{:S(2)}) %collective-permute-start.66) | collective-permute-done | bytes 4128 | tf_op jit(solution)/shard_map/ppermute | solution.py:21
  421.8 5.7 %collective-permute-done.67 = f32[4,2,128]{2,0,1:T(4,128)S(1)} collective-permute-done((f32[4,2,128]{2,0,1:T(4,128)S(1)}, f32[4,2,128]{2,0,1:T(4,128)S(1)}, u32[]{:S(2)}, u32[]{:S(2)}) %collective-permute-start.67) | collective-permute-done | bytes 4128 | tf_op jit(solution)/shard_map/ppermute | solution.py:21
  427.5 5.7 %collective-permute-done.68 = f32[4,2,128]{2,0,1:T(4,128)S(1)} collective-permute-done((f32[4,2,128]{2,0,1:T(4,128)S(1)}, f32[4,2,128]{2,0,1:T(4,128)S(1)}, u32[]{:S(2)}, u32[]{:S(2)}) %collective-permute-start.68) | collective-permute-done | bytes 4128 | tf_op jit(solution)/shard_map/ppermute | solution.py:21
  433.2 5.7 %collective-permute-done.69 = f32[4,2,128]{2,0,1:T(4,128)S(1)} collective-permute-done((f32[4,2,128]{2,0,1:T(4,128)S(1)}, f32[4,2,128]{2,0,1:T(4,128)S(1)}, u32[]{:S(2)}, u32[]{:S(2)}) %collective-permute-start.69) | collective-permute-done | bytes 4128 | tf_op jit(solution)/shard_map/ppermute | solution.py:21
  439.0 5.7 %collective-permute-done.70 = f32[4,2,128]{2,0,1:T(4,128)S(1)} collective-permute-done((f32[4,2,128]{2,0,1:T(4,128)S(1)}, f32[4,2,128]{2,0,1:T(4,128)S(1)}, u32[]{:S(2)}, u32[]{:S(2)}) %collective-permute-start.70) | collective-permute-done | bytes 4128 | tf_op jit(solution)/shard_map/ppermute | solution.py:21
  456.5 5.2 collective-permute-start.58
  469.8 6.6 %collective-permute-done.78 = f32[4,2,128]{2,0,1:T(4,128)S(1)} collective-permute-done((f32[4,2,128]{2,0,1:T(4,128)S(1)}, f32[4,2,128]{2,0,1:T(4,128)S(1)}, u32[]{:S(2)}, u32[]{:S(2)}) %collective-permute-start.78) | collective-permute-done | bytes 4128 | tf_op jit(solution)/shard_map/ppermute | solution.py:21
  476.4 5.7 %collective-permute-done.79 = f32[4,2,128]{2,0,1:T(4,128)S(1)} collective-permute-done((f32[4,2,128]{2,0,1:T(4,128)S(1)}, f32[4,2,128]{2,0,1:T(4,128)S(1)}, u32[]{:S(2)}, u32[]{:S(2)}) %collective-permute-start.79) | collective-permute-done | bytes 4128 | tf_op jit(solution)/shard_map/ppermute | solution.py:21
  482.1 5.7 %collective-permute-done.80 = f32[4,2,128]{2,0,1:T(4,128)S(1)} collective-permute-done((f32[4,2,128]{2,0,1:T(4,128)S(1)}, f32[4,2,128]{2,0,1:T(4,128)S(1)}, u32[]{:S(2)}, u32[]{:S(2)}) %collective-permute-start.80) | collective-permute-done | bytes 4128 | tf_op jit(solution)/shard_map/ppermute | solution.py:21
  487.8 5.7 %collective-permute-done.81 = f32[4,2,128]{2,0,1:T(4,128)S(1)} collective-permute-done((f32[4,2,128]{2,0,1:T(4,128)S(1)}, f32[4,2,128]{2,0,1:T(4,128)S(1)}, u32[]{:S(2)}, u32[]{:S(2)}) %collective-permute-start.81) | collective-permute-done | bytes 4128 | tf_op jit(solution)/shard_map/ppermute | solution.py:21
  493.5 5.7 %collective-permute-done.82 = f32[4,2,128]{2,0,1:T(4,128)S(1)} collective-permute-done((f32[4,2,128]{2,0,1:T(4,128)S(1)}, f32[4,2,128]{2,0,1:T(4,128)S(1)}, u32[]{:S(2)}, u32[]{:S(2)}) %collective-permute-start.82) | collective-permute-done | bytes 4128 | tf_op jit(solution)/shard_map/ppermute | solution.py:21
  499.3 5.7 %collective-permute-done.83 = f32[4,2,128]{2,0,1:T(4,128)S(1)} collective-permute-done((f32[4,2,128]{2,0,1:T(4,128)S(1)}, f32[4,2,128]{2,0,1:T(4,128)S(1)}, u32[]{:S(2)}, u32[]{:S(2)}) %collective-permute-start.83) | collective-permute-done | bytes 4128 | tf_op jit(solution)/shard_map/ppermute | solution.py:21
  505.0 5.7 %collective-permute-done.84 = f32[4,2,128]{2,0,1:T(4,128)S(1)} collective-permute-done((f32[4,2,128]{2,0,1:T(4,128)S(1)}, f32[4,2,128]{2,0,1:T(4,128)S(1)}, u32[]{:S(2)}, u32[]{:S(2)}) %collective-permute-start.84) | collective-permute-done | bytes 4128 | tf_op jit(solution)/shard_map/ppermute | solution.py:21
  511.0 5.7 %collective-permute-done.85 = f32[4,2,128]{2,0,1:T(4,128)S(1)} collective-permute-done((f32[4,2,128]{2,0,1:T(4,128)S(1)}, f32[4,2,128]{2,0,1:T(4,128)S(1)}, u32[]{:S(2)}, u32[]{:S(2)}) %collective-permute-start.85) | collective-permute-done | bytes 4128 | tf_op jit(solution)/shard_map/ppermute | solution.py:21
  516.7 5.7 %collective-permute-done.86 = f32[4,2,128]{2,0,1:T(4,128)S(1)} collective-permute-done((f32[4,2,128]{2,0,1:T(4,128)S(1)}, f32[4,2,128]{2,0,1:T(4,128)S(1)}, u32[]{:S(2)}, u32[]{:S(2)}) %collective-permute-start.86) | collective-permute-done | bytes 4128 | tf_op jit(solution)/shard_map/ppermute | solution.py:21
  522.4 5.7 %collective-permute-done.87 = f32[4,2,128]{2,0,1:T(4,128)S(1)} collective-permute-done((f32[4,2,128]{2,0,1:T(4,128)S(1)}, f32[4,2,128]{2,0,1:T(4,128)S(1)}, u32[]{:S(2)}, u32[]{:S(2)}) %collective-permute-start.87) | collective-permute-done | bytes 4128 | tf_op jit(solution)/shard_map/ppermute | solution.py:21
  528.2 5.7 %collective-permute-done.88 = f32[4,2,128]{2,0,1:T(4,128)S(1)} collective-permute-done((f32[4,2,128]{2,0,1:T(4,128)S(1)}, f32[4,2,128]{2,0,1:T(4,128)S(1)}, u32[]{:S(2)}, u32[]{:S(2)}) %collective-permute-start.88) | collective-permute-done | bytes 4128 | tf_op jit(solution)/shard_map/ppermute | solution.py:21
  533.9 5.7 %collective-permute-done.89 = f32[4,2,128]{2,0,1:T(4,128)S(1)} collective-permute-done((f32[4,2,128]{2,0,1:T(4,128)S(1)}, f32[4,2,128]{2,0,1:T(4,128)S(1)}, u32[]{:S(2)}, u32[]{:S(2)}) %collective-permute-start.89) | collective-permute-done | bytes 4128 | tf_op jit(solution)/shard_map/ppermute | solution.py:21
  551.4 5.2 collective-permute-start.77
  (296 shorter events, 120.8 us)
Async XLA Ops:
  7.2 139.4 %all-gather.2.cloned.1.call-start = ((), (), s32[]{:S(2)}) async-start(), calls=%async_computation | async-start | bytes 2228224 | tf_op jit(solution)/shard_map/all_gather | solution.py:127
  15.1 5.7 %collective-permute-start.4 = (f32[4,2,128]{2,0,1:T(4,128)S(1)}, f32[4,2,128]{2,0,1:T(4,128)S(1)}, u32[]{:S(2)}, u32[]{:S(2)}) collective-permute-start(f32[4,2,128]{2,0,1:T(4,128)S(1)} %collective-permute-done.3), channel_id=1, source_target_pairs={{0,1},{1,2},{2,3},{3,4},{4,5},{5,6},{6,7},{7,8},{8,9},{9,10},{10,1... | collective-permute-start | bytes 12296 | tf_op jit(solution)/shard_map/ppermute | solution.py:21
  20.9 5.7 %collective-permute-start.5 = (f32[4,2,128]{2,0,1:T(4,128)S(1)}, f32[4,2,128]{2,0,1:T(4,128)S(1)}, u32[]{:S(2)}, u32[]{:S(2)}) collective-permute-start(f32[4,2,128]{2,0,1:T(4,128)S(1)} %collective-permute-done.4), channel_id=1, source_target_pairs={{0,1},{1,2},{2,3},{3,4},{4,5},{5,6},{6,7},{7,8},{8,9},{9,10},{10,1... | collective-permute-start | bytes 12296 | tf_op jit(solution)/shard_map/ppermute | solution.py:21
  26.6 5.7 %collective-permute-start.6 = (f32[4,2,128]{2,0,1:T(4,128)S(1)}, f32[4,2,128]{2,0,1:T(4,128)S(1)}, u32[]{:S(2)}, u32[]{:S(2)}) collective-permute-start(f32[4,2,128]{2,0,1:T(4,128)S(1)} %collective-permute-done.5), channel_id=1, source_target_pairs={{0,1},{1,2},{2,3},{3,4},{4,5},{5,6},{6,7},{7,8},{8,9},{9,10},{10,1... | collective-permute-start | bytes 12296 | tf_op jit(solution)/shard_map/ppermute | solution.py:21
  32.3 5.7 %collective-permute-start.7 = (f32[4,2,128]{2,0,1:T(4,128)S(1)}, f32[4,2,128]{2,0,1:T(4,128)S(1)}, u32[]{:S(2)}, u32[]{:S(2)}) collective-permute-start(f32[4,2,128]{2,0,1:T(4,128)S(1)} %collective-permute-done.6), channel_id=1, source_target_pairs={{0,1},{1,2},{2,3},{3,4},{4,5},{5,6},{6,7},{7,8},{8,9},{9,10},{10,1... | collective-permute-start | bytes 12296 | tf_op jit(solution)/shard_map/ppermute | solution.py:21
  38.1 5.7 %collective-permute-start.8 = (f32[4,2,128]{2,0,1:T(4,128)S(1)}, f32[4,2,128]{2,0,1:T(4,128)S(1)}, u32[]{:S(2)}, u32[]{:S(2)}) collective-permute-start(f32[4,2,128]{2,0,1:T(4,128)S(1)} %collective-permute-done.7), channel_id=1, source_target_pairs={{0,1},{1,2},{2,3},{3,4},{4,5},{5,6},{6,7},{7,8},{8,9},{9,10},{10,1... | collective-permute-start | bytes 12296 | tf_op jit(solution)/shard_map/ppermute | solution.py:21
  43.8 5.7 %collective-permute-start.9 = (f32[4,2,128]{2,0,1:T(4,128)S(1)}, f32[4,2,128]{2,0,1:T(4,128)S(1)}, u32[]{:S(2)}, u32[]{:S(2)}) collective-permute-start(f32[4,2,128]{2,0,1:T(4,128)S(1)} %collective-permute-done.8), channel_id=1, source_target_pairs={{0,1},{1,2},{2,3},{3,4},{4,5},{5,6},{6,7},{7,8},{8,9},{9,10},{10,1... | collective-permute-start | bytes 12296 | tf_op jit(solution)/shard_map/ppermute | solution.py:21
  49.5 5.7 %collective-permute-start.10 = (f32[4,2,128]{2,0,1:T(4,128)S(1)}, f32[4,2,128]{2,0,1:T(4,128)S(1)}, u32[]{:S(2)}, u32[]{:S(2)}) collective-permute-start(f32[4,2,128]{2,0,1:T(4,128)S(1)} %collective-permute-done.9), channel_id=1, source_target_pairs={{0,1},{1,2},{2,3},{3,4},{4,5},{5,6},{6,7},{7,8},{8,9},{9,10},{10,1... | collective-permute-start | bytes 12296 | tf_op jit(solution)/shard_map/ppermute | solution.py:21
  55.2 5.7 %collective-permute-start.11 = (f32[4,2,128]{2,0,1:T(4,128)S(1)}, f32[4,2,128]{2,0,1:T(4,128)S(1)}, u32[]{:S(2)}, u32[]{:S(2)}) collective-permute-start(f32[4,2,128]{2,0,1:T(4,128)S(1)} %collective-permute-done.10), channel_id=1, source_target_pairs={{0,1},{1,2},{2,3},{3,4},{4,5},{5,6},{6,7},{7,8},{8,9},{9,10},{10,1... | collective-permute-start | bytes 12296 | tf_op jit(solution)/shard_map/ppermute | solution.py:21
  61.0 5.7 %collective-permute-start.12 = (f32[4,2,128]{2,0,1:T(4,128)S(1)}, f32[4,2,128]{2,0,1:T(4,128)S(1)}, u32[]{:S(2)}, u32[]{:S(2)}) collective-permute-start(f32[4,2,128]{2,0,1:T(4,128)S(1)} %collective-permute-done.11), channel_id=1, source_target_pairs={{0,1},{1,2},{2,3},{3,4},{4,5},{5,6},{6,7},{7,8},{8,9},{9,10},{10,1... | collective-permute-start | bytes 12296 | tf_op jit(solution)/shard_map/ppermute | solution.py:21
  61.0 38.3 %collective-permute-start.17 = (f32[4,1,128]{2,1,0:T(1,128)S(1)}, f32[4,1,128]{2,1,0:T(1,128)S(1)}, u32[]{:S(2)}, u32[]{:S(2)}) collective-permute-start(f32[4,1,128]{2,1,0:T(1,128)S(1)} %get-tuple-element.41), channel_id=1, source_target_pairs={{16,0},{17,1},{18,2},{19,3},{20,4},{21,5},{22,6},{23,7},{24,8},{25... | collective-permute-start | bytes 6152 | tf_op jit(solution)/shard_map/ppermute | solution.py:42
  62.7 36.6 %collective-permute-start.18 = (f32[4,1,128]{2,1,0:T(1,128)S(1)}, f32[4,1,128]{2,1,0:T(1,128)S(1)}, u32[]{:S(2)}, u32[]{:S(2)}) collective-permute-start(f32[4,1,128]{2,1,0:T(1,128)S(1)} %get-tuple-element.40), channel_id=1, source_target_pairs={{0,16},{1,17},{2,18},{3,19},{4,20},{5,21},{6,22},{7,23},{8,24},{9,... | collective-permute-start | bytes 6152 | tf_op jit(solution)/shard_map/ppermute | solution.py:40
  66.7 7.4 %collective-permute-start.13 = (f32[4,2,128]{2,0,1:T(4,128)S(1)}, f32[4,2,128]{2,0,1:T(4,128)S(1)}, u32[]{:S(2)}, u32[]{:S(2)}) collective-permute-start(f32[4,2,128]{2,0,1:T(4,128)S(1)} %collective-permute-done.12), channel_id=1, source_target_pairs={{0,1},{1,2},{2,3},{3,4},{4,5},{5,6},{6,7},{7,8},{8,9},{9,10},{10,1... | collective-permute-start | bytes 12296 | tf_op jit(solution)/shard_map/ppermute | solution.py:21
  69.1 30.3 %collective-permute-start = (f32[4,256,1]{2,1,0:T(8,128)}, f32[4,256,1]{2,1,0:T(8,128)S(1)}, u32[]{:S(2)}, u32[]{:S(2)}) collective-permute-start(f32[4,256,1]{2,1,0:T(8,128)} %get-tuple-element.42), channel_id=1, source_target_pairs={{1,0},{2,1},{3,2},{4,3},{5,4},{6,5},{7,6},{8,7},{9,8},{10,9},{11,1... | collective-permute-start | bytes 12296 | tf_op jit(solution)/shard_map/ppermute | solution.py:42
  74.1 25.2 %collective-permute-start.1 = (f32[4,256,1]{2,1,0:T(8,128)}, f32[4,256,1]{2,1,0:T(8,128)}, u32[]{:S(2)}, u32[]{:S(2)}) collective-permute-start(f32[4,256,1]{2,1,0:T(8,128)} %get-tuple-element.43), channel_id=1, source_target_pairs={{0,1},{1,2},{2,3},{3,4},{4,5},{5,6},{6,7},{7,8},{8,9},{9,10},{10,1... | collective-permute-start | bytes 12296 | tf_op jit(solution)/shard_map/ppermute | solution.py:40
  74.1 6.4 %collective-permute-start.14 = (f32[4,2,128]{2,0,1:T(4,128)S(1)}, f32[4,2,128]{2,0,1:T(4,128)S(1)}, u32[]{:S(2)}, u32[]{:S(2)}) collective-permute-start(f32[4,2,128]{2,0,1:T(4,128)S(1)} %collective-permute-done.13), channel_id=1, source_target_pairs={{0,1},{1,2},{2,3},{3,4},{4,5},{5,6},{6,7},{7,8},{8,9},{9,10},{10,1... | collective-permute-start | bytes 12296 | tf_op jit(solution)/shard_map/ppermute | solution.py:21
  80.6 10.3 %collective-permute-start.15 = (f32[4,2,128]{2,0,1:T(4,128)S(1)}, f32[4,2,128]{2,0,1:T(4,128)S(1)}, u32[]{:S(2)}, u32[]{:S(2)}) collective-permute-start(f32[4,2,128]{2,0,1:T(4,128)S(1)} %collective-permute-done.14), channel_id=1, source_target_pairs={{0,1},{1,2},{2,3},{3,4},{4,5},{5,6},{6,7},{7,8},{8,9},{9,10},{10,1... | collective-permute-start | bytes 12296 | tf_op jit(solution)/shard_map/ppermute | solution.py:21
  90.8 6.2 %collective-permute-start.16 = (f32[4,2,128]{2,0,1:T(4,128)S(1)}, f32[4,2,128]{2,0,1:T(4,128)S(1)}, u32[]{:S(2)}, u32[]{:S(2)}) collective-permute-start(f32[4,2,128]{2,0,1:T(4,128)S(1)} %collective-permute-done.15), channel_id=1, source_target_pairs={{0,1},{1,2},{2,3},{3,4},{4,5},{5,6},{6,7},{7,8},{8,9},{9,10},{10,1... | collective-permute-start | bytes 12296 | tf_op jit(solution)/shard_map/ppermute | solution.py:21
  197.4 5.7 %collective-permute-start.23 = (f32[4,2,128]{2,0,1:T(4,128)S(1)}, f32[4,2,128]{2,0,1:T(4,128)S(1)}, u32[]{:S(2)}, u32[]{:S(2)}) collective-permute-start(f32[4,2,128]{2,0,1:T(4,128)S(1)} %collective-permute-done.22), channel_id=1, source_target_pairs={{0,1},{1,2},{2,3},{3,4},{4,5},{5,6},{6,7},{7,8},{8,9},{9,10},{10,1... | collective-permute-start | bytes 12296 | tf_op jit(solution)/shard_map/ppermute | solution.py:21
  203.1 5.7 %collective-permute-start.24 = (f32[4,2,128]{2,0,1:T(4,128)S(1)}, f32[4,2,128]{2,0,1:T(4,128)S(1)}, u32[]{:S(2)}, u32[]{:S(2)}) collective-permute-start(f32[4,2,128]{2,0,1:T(4,128)S(1)} %collective-permute-done.23), channel_id=1, source_target_pairs={{0,1},{1,2},{2,3},{3,4},{4,5},{5,6},{6,7},{7,8},{8,9},{9,10},{10,1... | collective-permute-start | bytes 12296 | tf_op jit(solution)/shard_map/ppermute | solution.py:21
  208.9 5.7 %collective-permute-start.25 = (f32[4,2,128]{2,0,1:T(4,128)S(1)}, f32[4,2,128]{2,0,1:T(4,128)S(1)}, u32[]{:S(2)}, u32[]{:S(2)}) collective-permute-start(f32[4,2,128]{2,0,1:T(4,128)S(1)} %collective-permute-done.24), channel_id=1, source_target_pairs={{0,1},{1,2},{2,3},{3,4},{4,5},{5,6},{6,7},{7,8},{8,9},{9,10},{10,1... | collective-permute-start | bytes 12296 | tf_op jit(solution)/shard_map/ppermute | solution.py:21
  214.6 5.7 %collective-permute-start.26 = (f32[4,2,128]{2,0,1:T(4,128)S(1)}, f32[4,2,128]{2,0,1:T(4,128)S(1)}, u32[]{:S(2)}, u32[]{:S(2)}) collective-permute-start(f32[4,2,128]{2,0,1:T(4,128)S(1)} %collective-permute-done.25), channel_id=1, source_target_pairs={{0,1},{1,2},{2,3},{3,4},{4,5},{5,6},{6,7},{7,8},{8,9},{9,10},{10,1... | collective-permute-start | bytes 12296 | tf_op jit(solution)/shard_map/ppermute | solution.py:21
  220.3 5.7 %collective-permute-start.27 = (f32[4,2,128]{2,0,1:T(4,128)S(1)}, f32[4,2,128]{2,0,1:T(4,128)S(1)}, u32[]{:S(2)}, u32[]{:S(2)}) collective-permute-start(f32[4,2,128]{2,0,1:T(4,128)S(1)} %collective-permute-done.26), channel_id=1, source_target_pairs={{0,1},{1,2},{2,3},{3,4},{4,5},{5,6},{6,7},{7,8},{8,9},{9,10},{10,1... | collective-permute-start | bytes 12296 | tf_op jit(solution)/shard_map/ppermute | solution.py:21
  226.1 5.7 %collective-permute-start.28 = (f32[4,2,128]{2,0,1:T(4,128)S(1)}, f32[4,2,128]{2,0,1:T(4,128)S(1)}, u32[]{:S(2)}, u32[]{:S(2)}) collective-permute-start(f32[4,2,128]{2,0,1:T(4,128)S(1)} %collective-permute-done.27), channel_id=1, source_target_pairs={{0,1},{1,2},{2,3},{3,4},{4,5},{5,6},{6,7},{7,8},{8,9},{9,10},{10,1... | collective-permute-start | bytes 12296 | tf_op jit(solution)/shard_map/ppermute | solution.py:21
  231.8 5.7 %collective-permute-start.29 = (f32[4,2,128]{2,0,1:T(4,128)S(1)}, f32[4,2,128]{2,0,1:T(4,128)S(1)}, u32[]{:S(2)}, u32[]{:S(2)}) collective-permute-start(f32[4,2,128]{2,0,1:T(4,128)S(1)} %collective-permute-done.28), channel_id=1, source_target_pairs={{0,1},{1,2},{2,3},{3,4},{4,5},{5,6},{6,7},{7,8},{8,9},{9,10},{10,1... | collective-permute-start | bytes 12296 | tf_op jit(solution)/shard_map/ppermute | solution.py:21
  237.5 5.7 %collective-permute-start.30 = (f32[4,2,128]{2,0,1:T(4,128)S(1)}, f32[4,2,128]{2,0,1:T(4,128)S(1)}, u32[]{:S(2)}, u32[]{:S(2)}) collective-permute-start(f32[4,2,128]{2,0,1:T(4,128)S(1)} %collective-permute-done.29), channel_id=1, source_target_pairs={{0,1},{1,2},{2,3},{3,4},{4,5},{5,6},{6,7},{7,8},{8,9},{9,10},{10,1... | collective-permute-start | bytes 12296 | tf_op jit(solution)/shard_map/ppermute | solution.py:21
  243.2 5.7 %collective-permute-start.31 = (f32[4,2,128]{2,0,1:T(4,128)S(1)}, f32[4,2,128]{2,0,1:T(4,128)S(1)}, u32[]{:S(2)}, u32[]{:S(2)}) collective-permute-start(f32[4,2,128]{2,0,1:T(4,128)S(1)} %collective-permute-done.30), channel_id=1, source_target_pairs={{0,1},{1,2},{2,3},{3,4},{4,5},{5,6},{6,7},{7,8},{8,9},{9,10},{10,1... | collective-permute-start | bytes 12296 | tf_op jit(solution)/shard_map/ppermute | solution.py:21
  249.0 5.7 %collective-permute-start.32 = (f32[4,2,128]{2,0,1:T(4,128)S(1)}, f32[4,2,128]{2,0,1:T(4,128)S(1)}, u32[]{:S(2)}, u32[]{:S(2)}) collective-permute-start(f32[4,2,128]{2,0,1:T(4,128)S(1)} %collective-permute-done.31), channel_id=1, source_target_pairs={{0,1},{1,2},{2,3},{3,4},{4,5},{5,6},{6,7},{7,8},{8,9},{9,10},{10,1... | collective-permute-start | bytes 12296 | tf_op jit(solution)/shard_map/ppermute | solution.py:21
  249.0 25.8 %collective-permute-start.36 = (f32[4,1,128]{2,1,0:T(1,128)S(1)}, f32[4,1,128]{2,1,0:T(1,128)S(1)}, u32[]{:S(2)}, u32[]{:S(2)}) collective-permute-start(f32[4,1,128]{2,1,0:T(1,128)S(1)} %slice.260), channel_id=1, source_target_pairs={{0,16},{1,17},{2,18},{3,19},{4,20},{5,21},{6,22},{7,23},{8,24},{9,... | collective-permute-start | bytes 6152 | tf_op jit(solution)/shard_map/ppermute | solution.py:40
  250.3 24.5 %collective-permute-start.37 = (f32[4,1,128]{2,1,0:T(1,128)S(1)}, f32[4,1,128]{2,1,0:T(1,128)S(1)}, u32[]{:S(2)}, u32[]{:S(2)}) collective-permute-start(f32[4,1,128]{2,1,0:T(1,128)S(1)} %slice.259), channel_id=1, source_target_pairs={{16,0},{17,1},{18,2},{19,3},{20,4},{21,5},{22,6},{23,7},{24,8},{25... | collective-permute-start | bytes 6152 | tf_op jit(solution)/shard_map/ppermute | solution.py:42
  254.7 5.9 %collective-permute-start.33 = (f32[4,2,128]{2,0,1:T(4,128)S(1)}, f32[4,2,128]{2,0,1:T(4,128)S(1)}, u32[]{:S(2)}, u32[]{:S(2)}) collective-permute-start(f32[4,2,128]{2,0,1:T(4,128)S(1)} %collective-permute-done.32), channel_id=1, source_target_pairs={{0,1},{1,2},{2,3},{3,4},{4,5},{5,6},{6,7},{7,8},{8,9},{9,10},{10,1... | collective-permute-start | bytes 12296 | tf_op jit(solution)/shard_map/ppermute | solution.py:21
  266.4 6.2 %collective-permute-start.35 = (f32[4,2,128]{2,0,1:T(4,128)S(1)}, f32[4,2,128]{2,0,1:T(4,128)S(1)}, u32[]{:S(2)}, u32[]{:S(2)}) collective-permute-start(f32[4,2,128]{2,0,1:T(4,128)S(1)} %collective-permute-done.34), channel_id=1, source_target_pairs={{0,1},{1,2},{2,3},{3,4},{4,5},{5,6},{6,7},{7,8},{8,9},{9,10},{10,1... | collective-permute-start | bytes 12296 | tf_op jit(solution)/shard_map/ppermute | solution.py:21
  267.4 7.4 %collective-permute-start.19 = (f32[4,256,1]{2,1,0:T(8,128)}, f32[4,256,1]{2,1,0:T(8,128)}, u32[]{:S(2)}, u32[]{:S(2)}) collective-permute-start(f32[4,256,1]{2,1,0:T(8,128)} %get-tuple-element.36), channel_id=1, source_target_pairs={{0,1},{1,2},{2,3},{3,4},{4,5},{5,6},{6,7},{7,8},{8,9},{9,10},{10,1... | collective-permute-start | bytes 12296 | tf_op jit(solution)/shard_map/ppermute | solution.py:40
  267.4 9.2 %collective-permute-start.20 = (f32[4,256,1]{2,1,0:T(8,128)}, f32[4,256,1]{2,1,0:T(8,128)}, u32[]{:S(2)}, u32[]{:S(2)}) collective-permute-start(f32[4,256,1]{2,1,0:T(8,128)} %get-tuple-element.37), channel_id=1, source_target_pairs={{1,0},{2,1},{3,2},{4,3},{5,4},{6,5},{7,6},{8,7},{9,8},{10,9},{11,1... | collective-permute-start | bytes 12296 | tf_op jit(solution)/shard_map/ppermute | solution.py:42
  278.6 8.4 %collective-permute-start.40 = (f32[4,2,128]{2,0,1:T(4,128)S(1)}, f32[4,2,128]{2,0,1:T(4,128)S(1)}, u32[]{:S(2)}, u32[]{:S(2)}) collective-permute-start(f32[4,2,128]{2,0,1:T(4,128)S(1)} %pad_maximum_fusion.17), channel_id=1, source_target_pairs={{0,1},{1,2},{2,3},{3,4},{4,5},{5,6},{6,7},{7,8},{8,9},{9,10},{10,1... | collective-permute-start | bytes 12296 | tf_op jit(solution)/shard_map/ppermute | solution.py:21
  350.0 22.5 %collective-permute-start.55 = (f32[4,1,128]{2,1,0:T(1,128)S(1)}, f32[4,1,128]{2,1,0:T(1,128)S(1)}, u32[]{:S(2)}, u32[]{:S(2)}) collective-permute-start(f32[4,1,128]{2,1,0:T(1,128)S(1)} %get-tuple-element.31), channel_id=1, source_target_pairs={{0,16},{1,17},{2,18},{3,19},{4,20},{5,21},{6,22},{7,23},{8,24},{9,... | collective-permute-start | bytes 6152 | tf_op jit(solution)/shard_map/ppermute | solution.py:40
  351.3 21.2 %collective-permute-start.56 = (f32[4,1,128]{2,1,0:T(1,128)S(1)}, f32[4,1,128]{2,1,0:T(1,128)S(1)}, u32[]{:S(2)}, u32[]{:S(2)}) collective-permute-start(f32[4,1,128]{2,1,0:T(1,128)S(1)} %get-tuple-element.30), channel_id=1, source_target_pairs={{16,0},{17,1},{18,2},{19,3},{20,4},{21,5},{22,6},{23,7},{24,8},{25... | collective-permute-start | bytes 6152 | tf_op jit(solution)/shard_map/ppermute | solution.py:42
  355.7 5.9 %collective-permute-start.53 = (f32[4,2,128]{2,0,1:T(4,128)S(1)}, f32[4,2,128]{2,0,1:T(4,128)S(1)}, u32[]{:S(2)}, u32[]{:S(2)}) collective-permute-start(f32[4,2,128]{2,0,1:T(4,128)S(1)} %collective-permute-done.52), channel_id=1, source_target_pairs={{0,1},{1,2},{2,3},{3,4},{4,5},{5,6},{6,7},{7,8},{8,9},{9,10},{10,1... | collective-permute-start | bytes 12296 | tf_op jit(solution)/shard_map/ppermute | solution.py:21
  361.6 5.8 %collective-permute-start.54 = (f32[4,2,128]{2,0,1:T(4,128)S(1)}, f32[4,2,128]{2,0,1:T(4,128)S(1)}, u32[]{:S(2)}, u32[]{:S(2)}) collective-permute-start(f32[4,2,128]{2,0,1:T(4,128)S(1)} %collective-permute-done.53), channel_id=1, source_target_pairs={{0,1},{1,2},{2,3},{3,4},{4,5},{5,6},{6,7},{7,8},{8,9},{9,10},{10,1... | collective-permute-start | bytes 12296 | tf_op jit(solution)/shard_map/ppermute | solution.py:21
  361.7 10.8 %collective-permute-start.38 = (f32[4,256,1]{2,1,0:T(8,128)}, f32[4,256,1]{2,1,0:T(8,128)S(1)}, u32[]{:S(2)}, u32[]{:S(2)}) collective-permute-start(f32[4,256,1]{2,1,0:T(8,128)} %get-tuple-element.32), channel_id=1, source_target_pairs={{0,1},{1,2},{2,3},{3,4},{4,5},{5,6},{6,7},{7,8},{8,9},{9,10},{10,1... | collective-permute-start | bytes 12296 | tf_op jit(solution)/shard_map/ppermute | solution.py:40
  361.8 10.8 %collective-permute-start.39 = (f32[4,256,1]{2,1,0:T(8,128)}, f32[4,256,1]{2,1,0:T(8,128)}, u32[]{:S(2)}, u32[]{:S(2)}) collective-permute-start(f32[4,256,1]{2,1,0:T(8,128)} %get-tuple-element.33), channel_id=1, source_target_pairs={{1,0},{2,1},{3,2},{4,3},{5,4},{6,5},{7,6},{8,7},{9,8},{10,9},{11,1... | collective-permute-start | bytes 12296 | tf_op jit(solution)/shard_map/ppermute | solution.py:42
  375.0 6.6 %collective-permute-start.59 = (f32[4,2,128]{2,0,1:T(4,128)S(1)}, f32[4,2,128]{2,0,1:T(4,128)S(1)}, u32[]{:S(2)}, u32[]{:S(2)}) collective-permute-start(f32[4,2,128]{2,0,1:T(4,128)S(1)} %pad_maximum_fusion.18), channel_id=1, source_target_pairs={{0,1},{1,2},{2,3},{3,4},{4,5},{5,6},{6,7},{7,8},{8,9},{9,10},{10,1... | collective-permute-start | bytes 12296 | tf_op jit(solution)/shard_map/ppermute | solution.py:21
  387.4 5.7 %collective-permute-start.61 = (f32[4,2,128]{2,0,1:T(4,128)S(1)}, f32[4,2,128]{2,0,1:T(4,128)S(1)}, u32[]{:S(2)}, u32[]{:S(2)}) collective-permute-start(f32[4,2,128]{2,0,1:T(4,128)S(1)} %collective-permute-done.60), channel_id=1, source_target_pairs={{0,1},{1,2},{2,3},{3,4},{4,5},{5,6},{6,7},{7,8},{8,9},{9,10},{10,1... | collective-permute-start | bytes 12296 | tf_op jit(solution)/shard_map/ppermute | solution.py:21
  393.1 5.7 %collective-permute-start.62 = (f32[4,2,128]{2,0,1:T(4,128)S(1)}, f32[4,2,128]{2,0,1:T(4,128)S(1)}, u32[]{:S(2)}, u32[]{:S(2)}) collective-permute-start(f32[4,2,128]{2,0,1:T(4,128)S(1)} %collective-permute-done.61), channel_id=1, source_target_pairs={{0,1},{1,2},{2,3},{3,4},{4,5},{5,6},{6,7},{7,8},{8,9},{9,10},{10,1... | collective-permute-start | bytes 12296 | tf_op jit(solution)/shard_map/ppermute | solution.py:21
  398.8 5.7 %collective-permute-start.63 = (f32[4,2,128]{2,0,1:T(4,128)S(1)}, f32[4,2,128]{2,0,1:T(4,128)S(1)}, u32[]{:S(2)}, u32[]{:S(2)}) collective-permute-start(f32[4,2,128]{2,0,1:T(4,128)S(1)} %collective-permute-done.62), channel_id=1, source_target_pairs={{0,1},{1,2},{2,3},{3,4},{4,5},{5,6},{6,7},{7,8},{8,9},{9,10},{10,1... | collective-permute-start | bytes 12296 | tf_op jit(solution)/shard_map/ppermute | solution.py:21
  404.6 5.7 %collective-permute-start.64 = (f32[4,2,128]{2,0,1:T(4,128)S(1)}, f32[4,2,128]{2,0,1:T(4,128)S(1)}, u32[]{:S(2)}, u32[]{:S(2)}) collective-permute-start(f32[4,2,128]{2,0,1:T(4,128)S(1)} %collective-permute-done.63), channel_id=1, source_target_pairs={{0,1},{1,2},{2,3},{3,4},{4,5},{5,6},{6,7},{7,8},{8,9},{9,10},{10,1... | collective-permute-start | bytes 12296 | tf_op jit(solution)/shard_map/ppermute | solution.py:21
  410.3 5.7 %collective-permute-start.65 = (f32[4,2,128]{2,0,1:T(4,128)S(1)}, f32[4,2,128]{2,0,1:T(4,128)S(1)}, u32[]{:S(2)}, u32[]{:S(2)}) collective-permute-start(f32[4,2,128]{2,0,1:T(4,128)S(1)} %collective-permute-done.64), channel_id=1, source_target_pairs={{0,1},{1,2},{2,3},{3,4},{4,5},{5,6},{6,7},{7,8},{8,9},{9,10},{10,1... | collective-permute-start | bytes 12296 | tf_op jit(solution)/shard_map/ppermute | solution.py:21
  416.0 5.7 %collective-permute-start.66 = (f32[4,2,128]{2,0,1:T(4,128)S(1)}, f32[4,2,128]{2,0,1:T(4,128)S(1)}, u32[]{:S(2)}, u32[]{:S(2)}) collective-permute-start(f32[4,2,128]{2,0,1:T(4,128)S(1)} %collective-permute-done.65), channel_id=1, source_target_pairs={{0,1},{1,2},{2,3},{3,4},{4,5},{5,6},{6,7},{7,8},{8,9},{9,10},{10,1... | collective-permute-start | bytes 12296 | tf_op jit(solution)/shard_map/ppermute | solution.py:21
  421.8 5.7 %collective-permute-start.67 = (f32[4,2,128]{2,0,1:T(4,128)S(1)}, f32[4,2,128]{2,0,1:T(4,128)S(1)}, u32[]{:S(2)}, u32[]{:S(2)}) collective-permute-start(f32[4,2,128]{2,0,1:T(4,128)S(1)} %collective-permute-done.66), channel_id=1, source_target_pairs={{0,1},{1,2},{2,3},{3,4},{4,5},{5,6},{6,7},{7,8},{8,9},{9,10},{10,1... | collective-permute-start | bytes 12296 | tf_op jit(solution)/shard_map/ppermute | solution.py:21
  427.5 5.7 %collective-permute-start.68 = (f32[4,2,128]{2,0,1:T(4,128)S(1)}, f32[4,2,128]{2,0,1:T(4,128)S(1)}, u32[]{:S(2)}, u32[]{:S(2)}) collective-permute-start(f32[4,2,128]{2,0,1:T(4,128)S(1)} %collective-permute-done.67), channel_id=1, source_target_pairs={{0,1},{1,2},{2,3},{3,4},{4,5},{5,6},{6,7},{7,8},{8,9},{9,10},{10,1... | collective-permute-start | bytes 12296 | tf_op jit(solution)/shard_map/ppermute | solution.py:21
  444.7 22.5 %collective-permute-start.74 = (f32[4,1,128]{2,1,0:T(1,128)S(1)}, f32[4,1,128]{2,1,0:T(1,128)S(1)}, u32[]{:S(2)}, u32[]{:S(2)}) collective-permute-start(f32[4,1,128]{2,1,0:T(1,128)S(1)} %get-tuple-element.25), channel_id=1, source_target_pairs={{0,16},{1,17},{2,18},{3,19},{4,20},{5,21},{6,22},{7,23},{8,24},{9,... | collective-permute-start | bytes 6152 | tf_op jit(solution)/shard_map/ppermute | solution.py:40
  446.0 21.2 %collective-permute-start.75 = (f32[4,1,128]{2,1,0:T(1,128)S(1)}, f32[4,1,128]{2,1,0:T(1,128)S(1)}, u32[]{:S(2)}, u32[]{:S(2)}) collective-permute-start(f32[4,1,128]{2,1,0:T(1,128)S(1)} %get-tuple-element.24), channel_id=1, source_target_pairs={{16,0},{17,1},{18,2},{19,3},{20,4},{21,5},{22,6},{23,7},{24,8},{25... | collective-permute-start | bytes 6152 | tf_op jit(solution)/shard_map/ppermute | solution.py:42
  450.4 5.9 %collective-permute-start.72 = (f32[4,2,128]{2,0,1:T(4,128)S(1)}, f32[4,2,128]{2,0,1:T(4,128)S(1)}, u32[]{:S(2)}, u32[]{:S(2)}) collective-permute-start(f32[4,2,128]{2,0,1:T(4,128)S(1)} %collective-permute-done.71), channel_id=1, source_target_pairs={{0,1},{1,2},{2,3},{3,4},{4,5},{5,6},{6,7},{7,8},{8,9},{9,10},{10,1... | collective-permute-start | bytes 12296 | tf_op jit(solution)/shard_map/ppermute | solution.py:21
  456.3 5.8 %collective-permute-start.73 = (f32[4,2,128]{2,0,1:T(4,128)S(1)}, f32[4,2,128]{2,0,1:T(4,128)S(1)}, u32[]{:S(2)}, u32[]{:S(2)}) collective-permute-start(f32[4,2,128]{2,0,1:T(4,128)S(1)} %collective-permute-done.72), channel_id=1, source_target_pairs={{0,1},{1,2},{2,3},{3,4},{4,5},{5,6},{6,7},{7,8},{8,9},{9,10},{10,1... | collective-permute-start | bytes 12296 | tf_op jit(solution)/shard_map/ppermute | solution.py:21
  456.4 10.8 %collective-permute-start.57 = (f32[4,256,1]{2,1,0:T(8,128)}, f32[4,256,1]{2,1,0:T(8,128)S(1)}, u32[]{:S(2)}, u32[]{:S(2)}) collective-permute-start(f32[4,256,1]{2,1,0:T(8,128)} %get-tuple-element.26), channel_id=1, source_target_pairs={{0,1},{1,2},{2,3},{3,4},{4,5},{5,6},{6,7},{7,8},{8,9},{9,10},{10,1... | collective-permute-start | bytes 12296 | tf_op jit(solution)/shard_map/ppermute | solution.py:40
  456.5 10.8 %collective-permute-start.58 = (f32[4,256,1]{2,1,0:T(8,128)}, f32[4,256,1]{2,1,0:T(8,128)}, u32[]{:S(2)}, u32[]{:S(2)}) collective-permute-start(f32[4,256,1]{2,1,0:T(8,128)} %get-tuple-element.27), channel_id=1, source_target_pairs={{1,0},{2,1},{3,2},{4,3},{5,4},{6,5},{7,6},{8,7},{9,8},{10,9},{11,1... | collective-permute-start | bytes 12296 | tf_op jit(solution)/shard_map/ppermute | solution.py:42
  469.7 6.6 %collective-permute-start.78 = (f32[4,2,128]{2,0,1:T(4,128)S(1)}, f32[4,2,128]{2,0,1:T(4,128)S(1)}, u32[]{:S(2)}, u32[]{:S(2)}) collective-permute-start(f32[4,2,128]{2,0,1:T(4,128)S(1)} %pad_maximum_fusion.19), channel_id=1, source_target_pairs={{0,1},{1,2},{2,3},{3,4},{4,5},{5,6},{6,7},{7,8},{8,9},{9,10},{10,1... | collective-permute-start | bytes 12296 | tf_op jit(solution)/shard_map/ppermute | solution.py:21
  510.7 6.0 %collective-permute-start.85 = (f32[4,2,128]{2,0,1:T(4,128)S(1)}, f32[4,2,128]{2,0,1:T(4,128)S(1)}, u32[]{:S(2)}, u32[]{:S(2)}) collective-permute-start(f32[4,2,128]{2,0,1:T(4,128)S(1)} %collective-permute-done.84), channel_id=1, source_target_pairs={{0,1},{1,2},{2,3},{3,4},{4,5},{5,6},{6,7},{7,8},{8,9},{9,10},{10,1... | collective-permute-start | bytes 12296 | tf_op jit(solution)/shard_map/ppermute | solution.py:21
  539.6 22.5 %collective-permute-start.93 = (f32[4,1,128]{2,1,0:T(1,128)S(1)}, f32[4,1,128]{2,1,0:T(1,128)S(1)}, u32[]{:S(2)}, u32[]{:S(2)}) collective-permute-start(f32[4,1,128]{2,1,0:T(1,128)S(1)} %get-tuple-element.19), channel_id=1, source_target_pairs={{0,16},{1,17},{2,18},{3,19},{4,20},{5,21},{6,22},{7,23},{8,24},{9,... | collective-permute-start | bytes 6152 | tf_op jit(solution)/shard_map/ppermute | solution.py:40
  540.9 21.2 %collective-permute-start.94 = (f32[4,1,128]{2,1,0:T(1,128)S(1)}, f32[4,1,128]{2,1,0:T(1,128)S(1)}, u32[]{:S(2)}, u32[]{:S(2)}) collective-permute-start(f32[4,1,128]{2,1,0:T(1,128)S(1)} %get-tuple-element.18), channel_id=1, source_target_pairs={{16,0},{17,1},{18,2},{19,3},{20,4},{21,5},{22,6},{23,7},{24,8},{25... | collective-permute-start | bytes 6152 | tf_op jit(solution)/shard_map/ppermute | solution.py:42
  545.3 5.9 %collective-permute-start.91 = (f32[4,2,128]{2,0,1:T(4,128)S(1)}, f32[4,2,128]{2,0,1:T(4,128)S(1)}, u32[]{:S(2)}, u32[]{:S(2)}) collective-permute-start(f32[4,2,128]{2,0,1:T(4,128)S(1)} %collective-permute-done.90), channel_id=1, source_target_pairs={{0,1},{1,2},{2,3},{3,4},{4,5},{5,6},{6,7},{7,8},{8,9},{9,10},{10,1... | collective-permute-start | bytes 12296 | tf_op jit(solution)/shard_map/ppermute | solution.py:21
  551.2 5.8 %collective-permute-start.92 = (f32[4,2,128]{2,0,1:T(4,128)S(1)}, f32[4,2,128]{2,0,1:T(4,128)S(1)}, u32[]{:S(2)}, u32[]{:S(2)}) collective-permute-start(f32[4,2,128]{2,0,1:T(4,128)S(1)} %collective-permute-done.91), channel_id=1, source_target_pairs={{0,1},{1,2},{2,3},{3,4},{4,5},{5,6},{6,7},{7,8},{8,9},{9,10},{10,1... | collective-permute-start | bytes 12296 | tf_op jit(solution)/shard_map/ppermute | solution.py:21
  551.3 10.8 %collective-permute-start.76 = (f32[4,256,1]{2,1,0:T(8,128)}, f32[4,256,1]{2,1,0:T(8,128)S(1)}, u32[]{:S(2)}, u32[]{:S(2)}) collective-permute-start(f32[4,256,1]{2,1,0:T(8,128)} %get-tuple-element.20), channel_id=1, source_target_pairs={{0,1},{1,2},{2,3},{3,4},{4,5},{5,6},{6,7},{7,8},{8,9},{9,10},{10,1... | collective-permute-start | bytes 12296 | tf_op jit(solution)/shard_map/ppermute | solution.py:40
  551.4 10.8 %collective-permute-start.77 = (f32[4,256,1]{2,1,0:T(8,128)}, f32[4,256,1]{2,1,0:T(8,128)}, u32[]{:S(2)}, u32[]{:S(2)}) collective-permute-start(f32[4,256,1]{2,1,0:T(8,128)} %get-tuple-element.21), channel_id=1, source_target_pairs={{1,0},{2,1},{3,2},{4,3},{5,4},{6,5},{7,6},{8,7},{9,8},{10,9},{11,1... | collective-permute-start | bytes 12296 | tf_op jit(solution)/shard_map/ppermute | solution.py:42
  (40 other events, 296.9 us)
Sparse Core Ops, SparseCore 0:
  103.3 43.2 all-gather.1
